TPU v7x, 32 devices: a whole 2x2x4 slice. The times are simulated.
32 devices in a mesh: groups: 2 (over y), expert: 16 (over z, x, core), head: 1.
Axes of the slice: x: 2, y: 2, z: 4, core: 2. Of those that a mesh axis runs over, the one named last changes fastest.
Arguments:
- sources: bfloat16 [4096, 1024], P(('groups', 'expert')), parts along dimension 0, may hold values from -6 to 6
- enc_gain: float32 [1024], replicated, may hold values from 0.1 to 1.9
- route_ids: int32 [4096, 2], P(('groups', 'expert')), parts along dimension 0, may hold values from 0 to 7, all different within a row; in each aligned block of 128 rows (0 to 127, 128 to 255, ...) at most 40 rows name the same one
- route_gates: float32 [4096, 2], P(('groups', 'expert')), parts along dimension 0, may hold values from 0.2 to 1
- w_in: bfloat16 [16, 1024, 2048], P('expert', None, 'head'), may hold values from -0.1875 to 0.1875
- w_out: bfloat16 [16, 2048, 1024], P('expert', 'head'), may hold values from -0.09375 to 0.09375
- targets: bfloat16 [4096, 1024], P(('groups', 'expert')), parts along dimension 0, may hold values from -6 to 6
- dec_gain: float32 [1024], replicated, may hold values from 0.1 to 1.9
- src_lengths: int32 [64], P(('groups', 'expert')), parts along dimension 0, may hold values from 16 to 64, as said below
- tgt_lengths: int32 [64], P(('groups', 'expert')), parts along dimension 0, may hold values from 16 to 64, as said below
- w_query: bfloat16 [1024, 1024], P('expert', 'head'), may hold values from -60 to 60
- w_key: bfloat16 [1024, 1024], P('expert', 'head'), may hold values from -0.1875 to 0.1875
- w_value: bfloat16 [1024, 1024], P('expert', 'head'), may hold values from -0.1875 to 0.1875
- w_attn: bfloat16 [1024, 1024], P('expert', 'head'), may hold values from -0.1875 to 0.1875
Outputs:
- memory: bfloat16 [4096, 1024], P(('groups', 'expert')), parts along dimension 0
- decoded: bfloat16 [4096, 1024], P(('groups', 'expert'), 'head'), parts along dimension 0
There are 2 independent parts, one for each index of `groups`. A program takes and returns all parts, laid end to end along the dimension named above; an argument that names none is the same for every part. Nothing has to cross between parts.
Inputs may be any that keep to these rules, and one draw needn't show every extreme that they name: `route_ids`: in each aligned block of 128 rows no expert is named more than 40 times, a bound that some block reaches. `src_lengths`: some sentence has exactly 64 live tokens. `tgt_lengths`: some sentence has exactly 64 live tokens.
All inputs are finite; a program needn't handle non-finite values.
Results may differ from a plain program's by a relative error of at most 0.025.
Values may be sent and summed in bfloat16 or wider, within the bound.
No kernel may reach another device: no remote copies, remote signals or barrier semaphores. Data moves between devices by JAX's collectives and lax.ppermute only.
A program may use at most 64 MiB of HBM per device.

v0:
```python
import jax
import jax.numpy as jnp
from jax import lax
from jax.sharding import PartitionSpec as P

DH = 64


def from_partner(x, axis, stride):
    return lax.ppermute(x, axis, [(i, i ^ 1 << stride) for i in range(lax.axis_size(axis))])


def layer_norm(rows, gain):
    rows = rows.astype(jnp.float32)
    mean = jnp.mean(rows, axis=-1, keepdims=True)
    centered = rows - mean
    spread = jnp.mean(centered * centered, axis=-1, keepdims=True)
    return centered * lax.rsqrt(spread + 1e-05) * gain


def partner(block):
    return from_partner(block, "expert", 0)


def shards(
    sources,
    enc_gain,
    route_ids,
    route_gates,
    w_in,
    w_out,
    targets,
    dec_gain,
    src_lengths,
    tgt_lengths,
    w_query,
    w_key,
    w_value,
    w_attn,
):
    tok_rows, width = sources.shape
    experts = lax.axis_size("expert") // 2
    capacity = 2 * ((5 * tok_rows + 4 * experts - 1) // (4 * experts))
    side = lax.axis_index("expert") % 2
    pair_ids = route_ids.reshape(-1)
    onehot = (pair_ids[:, None] == jnp.arange(experts, dtype=jnp.int32)[None, :]).astype(jnp.int32)
    earlier = jnp.cumsum(onehot, axis=0) - onehot
    slots = jnp.sum(earlier * onehot, axis=1)
    place = pair_ids * capacity + slots
    normed = layer_norm(sources, enc_gain).astype(jnp.bfloat16)
    outgoing = (
        jnp.zeros((experts * capacity, width), jnp.bfloat16)
        .at[place]
        .set(jnp.repeat(normed, 2, axis=0))
    )
    sending = outgoing.reshape(2 * experts, capacity // 2, width)
    arrived = lax.all_to_all(sending, "expert", split_axis=0, concat_axis=0, tiled=True)
    other = partner(arrived)
    lower = jnp.where(side == 0, arrived, other)
    upper = jnp.where(side == 0, other, arrived)
    arrived = jnp.concatenate((lower, upper), axis=1)
    expert_rows = arrived.reshape(-1, width)
    hidden = jnp.maximum(
        jnp.dot(expert_rows, w_in[0], preferred_element_type=jnp.float32), 0.0
    ).astype(jnp.bfloat16)
    quarter = jnp.dot(hidden, w_out[0], preferred_element_type=jnp.float32)
    half = lax.psum(quarter.astype(jnp.bfloat16), "head")
    kept = half.shape[1]
    half = half.reshape(2 * experts, capacity, kept)
    other_half = partner(half)
    merged = (half.astype(jnp.float32) + other_half.astype(jnp.float32)).astype(jnp.bfloat16)
    leaving = lax.dynamic_slice_in_dim(merged, side * (capacity // 2), capacity // 2, 1)
    returned = lax.all_to_all(leaving, "expert", split_axis=0, concat_axis=0, tiled=True)
    results = returned.reshape(-1, kept)
    picked = jnp.take(results, place, axis=0).astype(jnp.float32).reshape(tok_rows, 2, kept)
    moe = route_gates[:, 0:1] * picked[:, 0, :] + route_gates[:, 1:2] * picked[:, 1, :]
    memory = (sources.astype(jnp.float32) + moe).astype(jnp.bfloat16)
    w_q, w_k, w_v, w_o = (
        lax.all_gather(w_query, "expert", axis=0, tiled=True),
        lax.all_gather(w_key, "expert", axis=0, tiled=True),
        lax.all_gather(w_value, "expert", axis=0, tiled=True),
        lax.all_gather(w_attn, "expert", axis=0, tiled=True),
    )
    tnormed = layer_norm(targets, dec_gain).astype(jnp.bfloat16)
    query = jnp.dot(tnormed, w_q, preferred_element_type=jnp.float32).astype(jnp.bfloat16)
    key = jnp.dot(memory, w_k, preferred_element_type=jnp.float32).astype(jnp.bfloat16)
    value = jnp.dot(memory, w_v, preferred_element_type=jnp.float32).astype(jnp.bfloat16)
    sentences = src_lengths.shape[0]
    local_heads = query.shape[1] // DH
    queries = query.reshape(sentences, -1, local_heads, DH)
    keys = key.reshape(sentences, -1, local_heads, DH)
    values = value.reshape(sentences, -1, local_heads, DH)
    key_count = keys.shape[1]
    scores = jnp.einsum(
        "sqhd,skhd->shqk", queries, keys, preferred_element_type=jnp.float32
    ) * DH ** (-0.5)
    live = jnp.arange(key_count, dtype=jnp.int32)[None, :] < src_lengths[:, None]
    scores = jnp.where(live[:, None, None, :], scores, -1e30)
    top = jnp.max(scores, axis=-1, keepdims=True)
    raised = jnp.exp(scores - top)
    weights = (raised / jnp.sum(raised, axis=-1, keepdims=True)).astype(jnp.bfloat16)
    context = jnp.einsum(
        "shqk,skhd->sqhd", weights, values, preferred_element_type=jnp.float32
    ).astype(jnp.bfloat16)
    context = context.reshape(targets.shape[0], -1)
    partial_out = lax.dot_general(
        context, w_o, (((1,), (1,)), ((), ())), preferred_element_type=jnp.float32
    )
    attn = lax.psum_scatter(
        partial_out.astype(jnp.bfloat16), "head", scatter_dimension=1, tiled=True
    ).astype(jnp.float32)
    share = width // lax.axis_size("head")
    own_targets = lax.dynamic_slice_in_dim(
        targets, lax.axis_index("head") * share, share, 1
    ).astype(jnp.float32)
    per_sentence = targets.shape[0] // sentences
    positions = jnp.arange(targets.shape[0], dtype=jnp.int32)
    owner = positions // per_sentence
    live_rows = (positions % per_sentence < jnp.take(tgt_lengths, owner)).astype(jnp.float32)
    decoded = ((own_targets + attn) * live_rows[:, None]).astype(jnp.bfloat16)
    return (memory, decoded)


def solution(mesh):
    placed = (
        P(("groups", "expert"), None),
        P(),
        P(("groups", "expert"), None),
        P(("groups", "expert"), None),
        P("expert", None, "head"),
        P("expert", "head", None),
        P(("groups", "expert"), None),
        P(),
        P(("groups", "expert")),
        P(("groups", "expert")),
        P("expert", "head"),
        P("expert", "head"),
        P("expert", "head"),
        P("expert", "head"),
    )
    return jax.shard_map(
        shards,
        mesh=mesh,
        in_specs=placed,
        out_specs=(P(("groups", "expert"), None), P(("groups", "expert"), "head")),
        check_vma=False,
    )
```

profile of v0, /device:TPU:0, one launch (start us, length us, event | category | flops | bytes accessed | tf_op | source)
XLA Modules:
  0.0 201.6 jit_solution(6229918482698029241)
XLA Ops:
  7.2 0.0 all-gather.7.cloned.1.call-start
  7.2 0.7 all-gather.7.cloned.1.call-update
  7.9 0.0 all-gather.5.cloned.1.call-start
  7.9 0.7 all-gather.5.cloned.1.call-update
  8.6 0.8 copy.44
  9.4 0.1 eq.34
  9.6 0.1 reshape.203
  9.7 0.7 broadcast_multiply_fusion
  10.4 0.1 copy.47
  10.5 0.1 mul.103
  10.7 0.6 reduce-window.6
  11.3 0.2 slice_reduce_fusion
  11.5 1.1 convert_reduce_fusion.1
  12.6 1.2 fusion.27
  13.8 1.2 fusion.29
  15.0 0.3 broadcast_in_dim.50
  15.2 0.2 reshape.235
  15.4 0.1 fusion.46
  15.5 1.9 scatter_custom_fusion
  17.4 1.0 reshape.206
  18.5 7.4 %all-to-all-start = ((bf16[16,20,1024]{2,1,0:T(8,128)(2,1)}), bf16[16,20,1024]{2,1,0:T(8,128)(2,1)S(1)}, u32[]{:S(2)}, u32[]{:S(2)}) async-start(bf16[16,20,1024]{2,1,0:T(8,128)(2,1)} %reshape.206), calls=%async_computation | async-start | bytes 1572864 | tf_op jit(solution)/shard_map/all_to_all | solution.py:57
  25.8 0.0 all-gather.9.cloned.1.call-start
  25.9 0.7 all-gather.9.cloned.1.call-update
  26.6 0.0 all-gather.11.cloned.1.call-start
  26.6 19.0 %all-to-all-done = bf16[16,20,1024]{2,1,0:T(8,128)(2,1)S(1)} async-done(((bf16[16,20,1024]{2,1,0:T(8,128)(2,1)}), bf16[16,20,1024]{2,1,0:T(8,128)(2,1)S(1)}, u32[]{:S(2)}, u32[]{:S(2)}) %all-to-all-start) | async-done | bytes 655392 | tf_op jit(solution)/shard_map/all_to_all | solution.py:57
  45.6 0.4 copy.48
  46.0 0.3 collective-permute-start
  46.3 1.9 collective-permute-done
  48.2 0.4 broadcast_select_fusion.1
  48.6 0.3 pad_maximum_fusion
  48.9 9.1 %fusion.7 = bf16[640,1024]{1,0:T(8,128)(2,1)S(1)} fusion(bf16[1,2048,1024]{2,1,0:T(8,128)(2,1)} %param.19, bf16[640,1024]{1,0:T(8,128)(2,1)S(1)} %bitcast.61, bf16[1,1024,2048]{2,1,0:T(8,128)(2,1)} %param.18), kind=kOutput, calls=%fused_computation.8 | convolution fusion | flops 5371985920 | bytes 11010048 | tf_op jit(solution)/shard_map/dot_general | solution.py:66
  58.0 0.3 collective-permute-start.1
  58.4 0.6 fusion.55
  59.0 0.1 convert_reduce_fusion
  59.1 0.2 fusion.24
  59.4 1.8 collective-permute-done.1
  61.1 1.5 add_convert_fusion
  62.6 11.7 %all-to-all-start.1 = ((bf16[16,20,1024]{2,1,0:T(8,128)(2,1)}), bf16[16,20,1024]{2,1,0:T(8,128)(2,1)S(1)}, u32[]{:S(2)}, u32[]{:S(2)}) async-start(bf16[16,20,1024]{2,1,0:T(8,128)(2,1)} %add_convert_fusion), calls=%async_computation.1 | async-start | bytes 1572864 | tf_op jit(solution)/shard_map/all_to_all | solution.py:73
  74.3 1.3 compare_convert_fusion
  75.7 0.1 reduce_sum.59
  75.8 0.1 copy.46
  75.9 0.1 iota_compare_fusion.2
  76.0 2.1 %convolution_convert_fusion.3 = bf16[128,1024]{1,0:T(8,128)(2,1)S(1)} fusion(bf16[1024,1024]{1,0:T(8,128)(2,1)} %all-gather.7.cloned.1.call-done, bf16[128,1024]{1,0:T(8,128)(2,1)S(1)} %copy-done, f32[1024]{0:T(1024)S(1)} %copy-done.4, f32[128]{0:T(128)S(1)} %add_rsqrt_fusion, f32[128]{0:T(128)S(1)} %broadcast_multiply_fusion.1), kind=kOutput, calls=%fused_computation.23 | convolution fusion | flops 269221888 | bytes 2626560 | tf_op jit(solution)/shard_map/dot_general | solution.py:85
  78.1 0.3 reshape.211
  78.5 15.5 %all-to-all-done.1 = bf16[16,20,1024]{2,1,0:T(8,128)(2,1)S(1)} async-done(((bf16[16,20,1024]{2,1,0:T(8,128)(2,1)}), bf16[16,20,1024]{2,1,0:T(8,128)(2,1)S(1)}, u32[]{:S(2)}, u32[]{:S(2)}) %all-to-all-start.1) | async-done | bytes 655392 | tf_op jit(solution)/shard_map/all_to_all | solution.py:73
  94.0 0.1 reshape.209
  94.1 1.2 gather_fusion
  95.3 0.2 gather.11
  95.5 0.2 fusion.37
  95.8 0.5 copy-done.1
  96.3 0.2 fusion.30
  96.4 10.8 %all-gather.5.cloned.1.call-done = bf16[1024,1024]{1,0:T(8,128)(2,1)} async-done(((bf16[64,1024]{1,0:T(8,128)(2,1)}), bf16[1024,1024]{1,0:T(8,128)(2,1)}) %all-gather.5.cloned.1.call-update) | async-done | bytes 2097168 | tf_op jit(solution)/shard_map/all_gather | solution.py:81
  107.3 2.0 %convolution_convert_fusion.4 = bf16[128,1024]{1,0:T(8,128)(2,1)S(1)} fusion(bf16[128,1024]{1,0:T(8,128)(2,1)S(1)} %fusion.30, bf16[1024,1024]{1,0:T(8,128)(2,1)} %all-gather.5.cloned.1.call-done), kind=kOutput, calls=%fused_computation.24 | convolution fusion | flops 268566528 | bytes 2621440 | tf_op jit(solution)/shard_map/dot_general | solution.py:87
  109.3 0.3 reshape.210
  109.7 40.1 %all-gather.9.cloned.1.call-done = bf16[1024,1024]{1,0:T(8,128)(2,1)} async-done(((bf16[64,1024]{1,0:T(8,128)(2,1)}), bf16[1024,1024]{1,0:T(8,128)(2,1)}) %all-gather.9.cloned.1.call-update) | async-done | bytes 2097168 | tf_op jit(solution)/shard_map/all_gather | solution.py:80
  149.8 2.0 %convolution_convert_fusion.2 = bf16[128,1024]{1,0:T(8,128)(2,1)S(1)} fusion(bf16[128,1024]{1,0:T(8,128)(2,1)S(1)} %fusion.30, bf16[1024,1024]{1,0:T(8,128)(2,1)} %all-gather.9.cloned.1.call-done), kind=kOutput, calls=%fused_computation.22 | convolution fusion | flops 268566528 | bytes 2621440 | tf_op jit(solution)/shard_map/dot_general | solution.py:86
  151.8 0.3 reshape.212
  152.2 0.6 fusion.56
  152.7 1.4 fusion.12
  154.1 2.0 %fusion.13 = bf16[2,64,16,64]{1,3,2,0:T(8,128)(2,1)S(1)} fusion(bf16[2,64,16,64]{3,2,1,0:T(8,128)(2,1)S(1)} %reshape.210, f32[2,16,64]{2,1,0:T(8,128)S(1)} %fusion.56, f32[2,16,64,64]{2,3,1,0:T(8,128)} %fusion.12), kind=kOutput, calls=%fused_computation.16 | convolution fusion | flops 17303616 | bytes 1056768 | tf_op jit(solution)/shard_map/shqk,skhd->sqhd/dot_general | solution.py:102
  156.2 0.4 copy.56
  156.6 0.3 reshape.213
  157.0 35.0 %all-gather.11.cloned.1.call-done = bf16[1024,1024]{1,0:T(8,128)(2,1)} async-done(((bf16[64,1024]{1,0:T(8,128)(2,1)}), bf16[1024,1024]{1,0:T(8,128)(2,1)}) %all-gather.11.cloned.1.call-update) | async-done | bytes 2097168 | tf_op jit(solution)/shard_map/all_gather | solution.py:82
  192.0 3.1 %fusion.17 = bf16[128,1024]{1,0:T(8,128)(2,1)} fusion(bf16[128,1024]{1,0:T(8,128)(2,1)S(1)} %reshape.213, bf16[1024,1024]{1,0:T(8,128)(2,1)} %all-gather.11.cloned.1.call-done, bf16[128,1024]{1,0:T(8,128)(2,1)S(1)} %copy-done, f32[128]{0:T(128)S(1)} %compare_convert_fusion), kind=kOutput, calls=%fused_computation.21 | convolution fusion | flops 269221888 | bytes 2884096 | tf_op jit(solution)/shard_map/dot_general | solution.py:106
  (28 shorter events, 0.2 us)
Async XLA Ops:
  7.2 68.9 %all-gather.7.cloned.1.call-start = ((), (), s32[]{:S(2)}) async-start(), calls=%async_computation.3 | async-start | bytes 2228224 | tf_op jit(solution)/shard_map/all_gather | solution.py:79
  7.9 99.4 %all-gather.5.cloned.1.call-start = ((), (), s32[]{:S(2)}) async-start(), calls=%async_computation.2 | async-start | bytes 2228224 | tf_op jit(solution)/shard_map/all_gather | solution.py:81
  18.5 27.2 %all-to-all-start = ((bf16[16,20,1024]{2,1,0:T(8,128)(2,1)}), bf16[16,20,1024]{2,1,0:T(8,128)(2,1)S(1)}, u32[]{:S(2)}, u32[]{:S(2)}) async-start(bf16[16,20,1024]{2,1,0:T(8,128)(2,1)} %reshape.206), calls=%async_computation | async-start | bytes 1572864 | tf_op jit(solution)/shard_map/all_to_all | solution.py:57
  25.8 123.9 %all-gather.9.cloned.1.call-start = ((), (), s32[]{:S(2)}) async-start(), calls=%async_computation.4 | async-start | bytes 2228224 | tf_op jit(solution)/shard_map/all_gather | solution.py:80
  26.6 165.4 %all-gather.11.cloned.1.call-start = ((), (), s32[]{:S(2)}) async-start(), calls=%async_computation.5 | async-start | bytes 2228224 | tf_op jit(solution)/shard_map/all_gather | solution.py:82
  46.0 2.2 %collective-permute-start = (bf16[16,20,1024]{2,0,1:T(8,128)(2,1)S(1)}, bf16[16,20,1024]{2,0,1:T(8,128)(2,1)S(1)}, u32[]{:S(2)}, u32[]{:S(2)}) collective-permute-start(bf16[16,20,1024]{2,0,1:T(8,128)(2,1)S(1)} %copy.48), channel_id=1, source_target_pairs={{0,1},{1,0},{2,3},{3,2},{4,5},{5,4},{6,7},{7,6},{8,9},{9,8},{10,11... | collective-permute-start | bytes 1966088 | tf_op jit(solution)/shard_map/ppermute | solution.py:10
  48.9 9.5 %copy-start.5 = (s32[2]{0:T(128)S(1)}, s32[2]{0:T(128)}, u32[]{:S(2)}) copy-start(s32[2]{0:T(128)} %param.23) | copy-start | bytes 28
  48.9 10.1 %copy-start = (bf16[128,1024]{1,0:T(8,128)(2,1)S(1)}, bf16[128,1024]{1,0:T(8,128)(2,1)}, u32[]{:S(2)}) copy-start(bf16[128,1024]{1,0:T(8,128)(2,1)} %param.20) | copy-start | bytes 786436
  58.0 3.1 %collective-permute-start.1 = (bf16[16,40,1024]{2,1,0:T(8,128)(2,1)S(1)}, bf16[16,40,1024]{2,1,0:T(8,128)(2,1)S(1)}, u32[]{:S(2)}, u32[]{:S(2)}) collective-permute-start(bf16[16,40,1024]{2,1,0:T(8,128)(2,1)S(1)} %bitcast.62), channel_id=1, source_target_pairs={{0,1},{1,0},{2,3},{3,2},{4,5},{5,4},{6,7},{7,6},{8,9},{9,8},{10,11... | collective-permute-start | bytes 3932168 | tf_op jit(solution)/shard_map/ppermute | solution.py:10
  59.3 16.6 %copy-start.7 = (s32[2]{0:T(128)S(1)}, s32[2]{0:T(128)}, u32[]{:S(2)}) copy-start(s32[2]{0:T(128)} %param.22) | copy-start | bytes 28
  59.3 16.6 %copy-start.6 = (f32[128,2]{0,1:T(2,128)S(1)}, f32[128,2]{0,1:T(2,128)}, u32[]{:S(2)}) copy-start(f32[128,2]{0,1:T(2,128)} %param.17) | copy-start | bytes 3076
  59.3 16.6 %copy-start.3 = (s32[128,2]{0,1:T(2,128)S(1)}, s32[128,2]{0,1:T(2,128)}, u32[]{:S(2)}) copy-start(s32[128,2]{0,1:T(2,128)} %param.16) | copy-start | bytes 3076
  59.3 16.7 %copy-start.4 = (f32[1024]{0:T(1024)S(1)}, f32[1024]{0:T(1024)}, u32[]{:S(2)}) copy-start(f32[1024]{0:T(1024)} %param.21) | copy-start | bytes 12292
  62.6 31.4 %all-to-all-start.1 = ((bf16[16,20,1024]{2,1,0:T(8,128)(2,1)}), bf16[16,20,1024]{2,1,0:T(8,128)(2,1)S(1)}, u32[]{:S(2)}, u32[]{:S(2)}) async-start(bf16[16,20,1024]{2,1,0:T(8,128)(2,1)} %add_convert_fusion), calls=%async_computation.1 | async-start | bytes 1572864 | tf_op jit(solution)/shard_map/all_to_all | solution.py:73
  95.3 1.0 copy-start.1
  96.4 55.4 %copy-start.2 = (bf16[128,1024]{1,0:T(8,128)(2,1)}, bf16[128,1024]{1,0:T(8,128)(2,1)S(1)}, u32[]{:S(2)}) copy-start(bf16[128,1024]{1,0:T(8,128)(2,1)S(1)} %fusion.30) | copy-start | bytes 786436
Sparse Core Ops, SparseCore 0:
  10.2 49.3 all-gather.6
  61.7 45.5 all-gather.4
  109.4 40.2 all-gather.8
  151.8 40.1 all-gather.10
where the time goes:
time: 202 us
  waiting for transfers between devices  126 us (62%)
  matrix products  22.4 us (11%)
  starting transfers between devices  19.8 us (10%)
  between operations  14.1 us (7%)
  local copies, waits for them, and re-layouts  9.9 us (5%)
  other arithmetic  9.17 us (5%)
    all_gather x1, waiting for transfers between devices, shards(): lax.all_gather(w_key, 'expert', axis=0, tiled=True)  40.1 us
    all_gather x1, waiting for transfers between devices, shards(): lax.all_gather(w_attn, 'expert', axis=0, tiled=True)  35 us
    all_to_all x1, waiting for transfers between devices, shards(): lax.all_to_all(sending, 'expert', split_axis=0, concat_axis=0, tiled=True)  19 us
    all_to_all x1, waiting for transfers between devices, shards(): lax.all_to_all(leaving, 'expert', split_axis=0, concat_axis=0, tiled=True)  15.5 us
    all_to_all x1, starting transfers between devices, shards(): lax.all_to_all(leaving, 'expert', split_axis=0, concat_axis=0, tiled=True)  11.7 us
    all_gather x1, waiting for transfers between devices, shards(): lax.all_gather(w_value, 'expert', axis=0, tiled=True)  10.8 us
    dot_general x1, matrix products, shards(): quarter = jnp.dot(hidden, w_out[0], preferred_element_type=jnp.float32)  9.11 us
    all_to_all x1, starting transfers between devices, shards(): lax.all_to_all(sending, 'expert', split_axis=0, concat_axis=0, tiled=True)  7.36 us
  transfers between devices with their start and end apart: 8, of which 7 were waited for; matrix products, arithmetic and copies ran while one was open for 19% of the time, Pallas kernels for 0%

commit v1 on v0

v1 whole, which is shorter than its diff:
```python
import functools

import jax
import jax.numpy as jnp
from jax import lax
from jax.experimental import pallas as pl
from jax.experimental.pallas import tpu as pltpu
from jax.sharding import Mesh, PartitionSpec as P

DH = 64
F32, BF16 = jnp.float32, jnp.bfloat16
CHIPS = ("hi", "lo")
EXPERT = ("hi", "lo", "pair")
VMEM_LIMIT = 48 * 2**20


def layer_norm(rows, gain):
    rows = rows.astype(F32)
    mean = jnp.mean(rows, axis=-1, keepdims=True)
    centered = rows - mean
    spread = jnp.mean(centered * centered, axis=-1, keepdims=True)
    return centered * lax.rsqrt(spread + 1e-05) * gain


def places(ids, experts, capacity):
    tokens = ids.shape[0]
    lanes = -(-experts // 128) * 128
    expert = lax.broadcasted_iota(jnp.int32, (tokens, lanes), 1)
    first, second = (
        jnp.where(expert == ids[:, j : j + 1], 1.0, 0.0).astype(F32) for j in range(2)
    )
    row = lax.broadcasted_iota(jnp.int32, (tokens, tokens), 0)
    col = lax.broadcasted_iota(jnp.int32, (tokens, tokens), 1)
    before = jnp.where(col < row, 1.0, 0.0).astype(BF16)
    earlier = jnp.dot(before, (first + second).astype(BF16), preferred_element_type=F32)
    slots = (
        jnp.sum(earlier * first, axis=1, keepdims=True),
        jnp.sum((earlier + first) * second, axis=1, keepdims=True),
    )
    return [
        ids[:, j : j + 1].astype(F32) * capacity + slots[j] for j in range(2)
    ]


def prep_kernel(experts, capacity, sources, gain, ids, out):
    tokens = sources.shape[0]
    first, second = places(ids[...], experts, capacity)
    normed = layer_norm(sources[...], gain[...]).astype(BF16)
    slot = lax.broadcasted_iota(jnp.int32, (out.shape[0], tokens), 0).astype(F32)
    across = [jnp.transpose(jnp.broadcast_to(p, (tokens, tokens)))[0:1] for p in (first, second)]
    pick = jnp.where((slot == across[0]) | (slot == across[1]), 1.0, 0.0).astype(BF16)
    out[...] = jnp.dot(pick, normed, preferred_element_type=F32).astype(BF16)


def query_kernel(experts, capacity, targets, gain, ids, gates, w_q, query, high, low):
    tnormed = layer_norm(targets[...], gain[...]).astype(BF16)
    depth = tnormed.shape[1]
    weight = w_q[...].reshape(depth, -1)
    query[...] = jnp.dot(tnormed, weight, preferred_element_type=F32).astype(BF16)
    first, second = places(ids[...], experts, capacity)
    slot = lax.broadcasted_iota(jnp.int32, high.shape, 1).astype(F32)
    mix = jnp.where(slot == first, gates[:, 0:1], 0.0) + jnp.where(slot == second, gates[:, 1:2], 0.0)
    top = mix.astype(BF16)
    high[...] = top
    low[...] = (mix - top.astype(F32)).astype(BF16)


def ffn_kernel(rows, in_a, in_b, out_a, out_b, out, total):
    step = pl.program_id(0)

    @pl.when(step == 0)
    def _():
        total[...] = jnp.zeros_like(total)

    part = None
    for first, second in ((in_a, out_a), (in_b, out_b)):
        hidden = jnp.dot(rows[...], first[0], preferred_element_type=F32)
        hidden = jnp.maximum(hidden, 0.0).astype(BF16)
        term = jnp.dot(hidden, second[0], preferred_element_type=F32)
        part = term if part is None else part + term
    total[...] += part

    @pl.when(step == pl.num_programs(0) - 1)
    def _():
        out[...] = total[...].astype(BF16)


def memory_of(results, high, low, sources):
    moe = jnp.dot(high, results, preferred_element_type=F32) + jnp.dot(low, results, preferred_element_type=F32)
    return (sources.astype(F32) + moe).astype(BF16)


def attend(query, key, value, lengths, sentences):
    q_rows, k_rows = query.shape[0] // sentences, key.shape[0] // sentences
    both = 2 * DH
    lane = lax.broadcasted_iota(jnp.int32, (query.shape[0], both), 1)
    row = lax.broadcasted_iota(jnp.int32, (query.shape[0], key.shape[0]), 0)
    col = lax.broadcasted_iota(jnp.int32, (query.shape[0], key.shape[0]), 1)
    live = jnp.zeros(row.shape, jnp.bool_)
    for s in range(sentences):
        live = live | (
            (row >= s * q_rows) & (row < (s + 1) * q_rows)
            & (col >= s * k_rows) & (col < s * k_rows + jnp.minimum(lengths[s], k_rows))
        )
    live = jnp.concatenate((live, live), axis=0)
    contexts = []
    for pair in range(query.shape[1] // both):
        columns = slice(pair * both, (pair + 1) * both)
        q = query[:, columns]
        zero = jnp.zeros_like(q)
        q = jnp.concatenate((jnp.where(lane < DH, q, zero), jnp.where(lane < DH, zero, q)), axis=0)
        scores = lax.dot_general(q, key[:, columns], (((1,), (1,)), ((), ())), preferred_element_type=F32)
        scores = jnp.where(live, scores * DH ** (-0.5), -1e30)
        raised = jnp.exp(scores - jnp.max(scores, axis=-1, keepdims=True))
        weights = (raised / jnp.sum(raised, axis=-1, keepdims=True)).astype(BF16)
        mixed = jnp.dot(weights, value[:, columns], preferred_element_type=F32)
        half = query.shape[0]
        contexts.append(jnp.where(lane < DH, mixed[:half], mixed[half:]).astype(BF16))
    return jnp.concatenate(contexts, axis=1)


def tail_kernel(
    sentences, src_lengths, results, high, low, sources, query, w_k, w_v, w_o, memory, partial_out
):
    mem = memory_of(results[...], high[...], low[...], sources[...])
    memory[...] = mem
    depth = mem.shape[1]
    key = jnp.dot(mem, w_k[...].reshape(depth, -1), preferred_element_type=F32).astype(BF16)
    value = jnp.dot(mem, w_v[...].reshape(depth, -1), preferred_element_type=F32).astype(BF16)
    context = attend(query[...], key, value, src_lengths, sentences)
    partial_out[...] = lax.dot_general(
        context, w_o[...].reshape(depth, -1), (((1,), (1,)), ((), ())), preferred_element_type=F32
    ).astype(partial_out.dtype)


def live_rows(count, lengths, sentences):
    row = lax.broadcasted_iota(jnp.int32, (count, 1), 0)
    each = count // sentences
    live = jnp.zeros((count, 1), jnp.bool_)
    for s in range(sentences):
        live = live | ((row >= s * each) & (row < s * each + jnp.minimum(lengths[s], each)))
    return jnp.where(live, 1.0, 0.0)


def tail_whole_kernel(
    sentences, src_lengths, tgt_lengths, results, high, low, sources, query, targets,
    w_k, w_v, w_o, memory, decoded, attn
):
    tail_kernel(
        sentences, src_lengths, results, high, low, sources, query, w_k, w_v, w_o, memory, attn
    )
    live = live_rows(targets.shape[0], tgt_lengths, sentences)
    decoded[...] = ((targets[...].astype(F32) + attn[...]) * live).astype(BF16)


def whole(shape, dtype=BF16):
    return jax.ShapeDtypeStruct(shape, dtype)


def vmem(count):
    return [pl.BlockSpec(memory_space=pltpu.VMEM)] * count


def smem(count):
    return [pl.BlockSpec(memory_space=pltpu.SMEM)] * count


PARAMS = pltpu.CompilerParams(vmem_limit_bytes=VMEM_LIMIT)


def ffn(rows, in_a, in_b, out_a, out_b):
    depth, units = in_a.shape[1:]
    block = min(units, 256)
    count, width = rows.shape[0], out_a.shape[2]
    fixed = pl.BlockSpec((count, depth), lambda i: (0, 0))
    first = pl.BlockSpec((1, depth, block), lambda i: (0, 0, i))
    second = pl.BlockSpec((1, block, width), lambda i: (0, i, 0))
    return pl.pallas_call(
        ffn_kernel,
        grid=(units // block,),
        in_specs=[fixed, first, first, second, second],
        out_specs=pl.BlockSpec((count, width), lambda i: (0, 0)),
        out_shape=whole((count, width)),
        scratch_shapes=[pltpu.VMEM((count, width), F32)],
        compiler_params=PARAMS,
        cost_estimate=pl.CostEstimate(
            flops=8 * count * depth * units, bytes_accessed=8 * depth * units, transcendentals=0
        ),
    )(rows, in_a, in_b, out_a, out_b)


def partner(block):
    return lax.ppermute(block, "pair", [(0, 1), (1, 0)])


def weight_spec(gathered, index):
    shape = gathered.shape
    return pl.BlockSpec((shape[0], 1, *shape[2:]), lambda i: (0, index, 0, 0))


def shards(
    sources,
    enc_gain,
    route_ids,
    route_gates,
    w_in,
    w_out,
    targets,
    dec_gain,
    src_lengths,
    tgt_lengths,
    w_query,
    w_key,
    w_value,
    w_attn,
):
    tokens, width = sources.shape
    experts = lax.axis_size("hi") * lax.axis_size("lo")
    heads = lax.axis_size("head")
    capacity = 2 * ((5 * tokens + 4 * experts - 1) // (4 * experts))
    sentences = src_lengths.shape[0]
    enc_gain, dec_gain = enc_gain.reshape(1, -1), dec_gain.reshape(1, -1)

    stacked = jnp.stack((w_query, w_key, w_value, w_attn))
    gathered = lax.all_gather(stacked, EXPERT, axis=0, tiled=False)
    other_in, other_out = partner(w_in), partner(w_out)

    outgoing = pl.pallas_call(
        functools.partial(prep_kernel, experts, capacity),
        in_specs=vmem(3),
        out_specs=vmem(1)[0],
        out_shape=whole((experts * capacity, width)),
        compiler_params=PARAMS,
    )(sources, enc_gain, route_ids)
    arrived = lax.all_to_all(
        outgoing.reshape(experts, capacity, width), CHIPS, split_axis=0, concat_axis=0, tiled=True
    ).reshape(-1, width)
    half = ffn(arrived, w_in, other_in, w_out, other_out)
    if heads > 1:
        half = lax.psum(half.astype(F32), "head").astype(BF16)
    results = lax.all_to_all(
        half.reshape(experts, capacity, width), CHIPS, split_axis=0, concat_axis=0, tiled=True
    ).reshape(-1, width)

    columns = w_query.shape[1]
    query, high, low = pl.pallas_call(
        functools.partial(query_kernel, experts, capacity),
        grid=(1,),
        in_specs=vmem(4) + [weight_spec(gathered, 0)],
        out_specs=vmem(3),
        out_shape=(
            whole((targets.shape[0], columns)),
            whole((tokens, experts * capacity)),
            whole((tokens, experts * capacity)),
        ),
        compiler_params=PARAMS,
    )(targets, dec_gain, route_ids, route_gates, gathered)

    weights = [weight_spec(gathered, i) for i in (1, 2, 3)]
    if heads == 1:
        return pl.pallas_call(
            functools.partial(tail_whole_kernel, sentences),
            grid=(1,),
            in_specs=smem(2) + vmem(6) + weights,
            out_specs=vmem(2),
            out_shape=(whole(sources.shape), whole(targets.shape)),
            scratch_shapes=[pltpu.VMEM(targets.shape, F32)],
            compiler_params=PARAMS,
        )(
            src_lengths, tgt_lengths, results, high, low, sources, query, targets,
            gathered, gathered, gathered,
        )
    memory, partial_out = pl.pallas_call(
        functools.partial(tail_kernel, sentences),
        grid=(1,),
        in_specs=smem(1) + vmem(5) + weights,
        out_specs=vmem(2),
        out_shape=(whole(sources.shape), whole(targets.shape)),
        compiler_params=PARAMS,
    )(src_lengths, results, high, low, sources, query, gathered, gathered, gathered)
    attn = lax.psum_scatter(partial_out, "head", scatter_dimension=1, tiled=True).astype(F32)
    share = width // heads
    own = lax.dynamic_slice_in_dim(targets, lax.axis_index("head") * share, share, 1).astype(F32)
    each = targets.shape[0] // sentences
    positions = jnp.arange(targets.shape[0], dtype=jnp.int32)
    live = (positions % each < jnp.take(tgt_lengths, positions // each)).astype(F32)
    return memory, ((own + attn) * live[:, None]).astype(BF16)


def solution(mesh):
    groups, experts, heads = (mesh.shape[name] for name in ("groups", "expert", "head"))
    chips = experts // 2
    low = 2 if chips % 2 == 0 else 1
    fine = Mesh(
        mesh.devices.reshape(groups, chips // low, low, 2, heads),
        ("groups", "hi", "lo", "pair", "head"),
    )
    rows = ("groups", "hi", "lo", "pair")
    placed = (
        P(rows, None),
        P(),
        P(rows, None),
        P(rows, None),
        P(EXPERT, None, "head"),
        P(EXPERT, "head", None),
        P(rows, None),
        P(),
        P(rows),
        P(rows),
        P(EXPERT, "head"),
        P(EXPERT, "head"),
        P(EXPERT, "head"),
        P(EXPERT, "head"),
    )
    return jax.shard_map(
        shards,
        mesh=fine,
        in_specs=placed,
        out_specs=(P(rows, None), P(rows, "head")),
        check_vma=False,
    )
```

time: 202 us -> 128 us (0.63)
  waiting for transfers between devices: 126 us -> 41.2 us
  blocking collectives: 0 us -> 39.8 us
  matrix products: 22.4 us -> 0 us
  Pallas kernels: 0 us -> 21.4 us
  starting transfers between devices: 19.8 us -> 4.18 us
  other arithmetic: 9.17 us -> 1.97 us
  local copies, waits for them, and re-layouts: 9.9 us -> 4.74 us
    all_gather x4 -> x1, waiting for transfers between devices: 85.9 us -> 41.2 us  [shards(): gathered = lax.all_gather(stacked, EXPERT, axis=0, tiled=False)]
    all_to_all x0 -> x1, blocking collectives: none -> 39.8 us  [shards(): lax.all_to_all(outgoing.reshape(experts, capacity, width), CHIPS, split_a...]
    all_to_all x2 -> x1, waiting for transfers between devices: 34.6 us -> 0.01 us  [shards(): lax.all_to_all(half.reshape(experts, capacity, width), CHIPS, split_axis=...]
    dot_general x7 -> x0, matrix products: 21.8 us -> none  [the longest x1 9.11 us: shards(): quarter = jnp.dot(hidden, w_out[0], preferred_element_type=jnp.float32)]
    pallas_call x0 -> x4, Pallas kernels: none -> 21.4 us  [the longest x1 12.1 us: ffn(): pl.pallas_call(ffn_kernel, grid=(units // block,), in_specs=[fixed, first...]
    all_to_all x2 -> x1, starting transfers between devices: 19.1 us -> 3.54 us  [shards(): lax.all_to_all(half.reshape(experts, capacity, width), CHIPS, split_axis=...]
    convert_element_type x6 -> x0, other arithmetic: 4.36 us -> none  [the longest x1 1.49 us: shards(): (half.astype(jnp.float32) + other_half.astype(jnp.float32)).astype(jnp.bf...]
    ppermute x2, waiting for transfers between devices: 3.64 us -> 0.01 us  [partner(): return lax.ppermute(block, 'pair', [(0, 1), (1, 0)])]
  transfers between devices with their start and end apart: 8 -> 4, of which waited for: 7 -> 1; matrix products, arithmetic and copies ran while one was open for 19% -> 1% of each run, Pallas kernels for 0% -> 12%
where the time goes in v1:
time: 128 us; the launch traced here: 127 us
  waiting for transfers between devices  41.2 us (32%)
  blocking collectives  39.8 us (31%)
  Pallas kernels  21.4 us (17%)
  between operations  14.1 us (11%)
  local copies, waits for them, and re-layouts  4.74 us (4%)
  starting transfers between devices  4.18 us (3%)
  other arithmetic  1.97 us (2%)
    all_gather x1, waiting for transfers between devices, shards(): gathered = lax.all_gather(stacked, EXPERT, axis=0, tiled=False)  41.2 us
    all_to_all x1, blocking collectives, shards(): lax.all_to_all(outgoing.reshape(experts, capacity, width), CHIPS, split_a...  39.8 us
    pallas_call x1, Pallas kernels, ffn(): pl.pallas_call(ffn_kernel, grid=(units // block,), in_specs=[fixed, first...  12.1 us
    pallas_call x1, Pallas kernels, shards(): pl.pallas_call(functools.partial(tail_whole_kernel, sentences), grid=(1,)...  5.95 us
    unnamed x20, local copies, waits for them, and re-layouts  4.74 us
    all_to_all x1, starting transfers between devices, shards(): lax.all_to_all(half.reshape(experts, capacity, width), CHIPS, split_axis=...  3.54 us
  transfers between devices with their start and end apart: 4, of which 1 were waited for; matrix products, arithmetic and copies ran while one was open for 1% of the time, Pallas kernels for 12%

profile of v1, /device:TPU:0, one launch (start us, length us, event | category | flops | bytes accessed | tf_op | source)
XLA Modules:
  0.0 127.4 jit_solution(3650092231120406124)
XLA Ops:
  7.2 0.0 all-gather.3.cloned.1.call-start
  7.2 2.0 %pad_maximum_fusion = bf16[4,64,1024]{2,1,0:T(8,128)(2,1)} fusion(bf16[1,64,1024]{2,1,0:T(8,128)(2,1)} %bitcast.20, bf16[1,64,1024]{2,1,0:T(8,128)(2,1)} %bitcast.21, bf16[1,64,1024]{2,1,0:T(8,128)(2,1)} %bitcast.22, bf16[1,64,1024]{2,1,0:T(8,128)(2,1)} %bitcast.23), kind=kLoop, calls=%fused_computation | loop fusion | flops 786432 | bytes 1048576 | tf_op jit(solution)/shard_map/stack | solution.py:224
  9.2 0.0 all-gather.3.cloned.1.call-update
  9.2 0.5 collective-permute-start
  9.7 0.1 collective-permute-start.1
  9.8 0.8 copy.19.ids
  10.6 0.0 copy-start.1
  10.6 0.9 copy-done.1
  11.5 0.0 copy-start.3
  11.5 0.7 copy-done.3
  12.2 0.8 shard_map.149
  13.1 39.8 %all_to_all.10 = bf16[8,40,1024]{2,1,0:T(8,128)(2,1)S(1)} all-to-all(bf16[8,40,1024]{2,1,0:T(8,128)(2,1)S(1)} %bitcast.11), channel_id=1, replica_groups=mesh['groups'=2,'hi'=4,'lo'=2,'pair'=2,'head'=1] {'hi','lo'}, dimensions={0} | all-to-all | bytes 1310720 | tf_op jit(solution)/shard_map/all_to_all | solution.py:235
  52.9 0.0 collective-permute-done.in_b
  52.9 0.0 collective-permute-done.1.out_b
  52.9 0.0 copy-start.7
  52.9 2.2 %copy-done.7 = bf16[1,1024,2048]{2,1,0:T(8,128)(2,1)S(1)} copy-done((bf16[1,1024,2048]{2,1,0:T(8,128)(2,1)S(1)}, bf16[1,1024,2048]{2,1,0:T(8,128)(2,1)}, u32[]{:S(2)}) %copy-start.7) | copy-done | bytes 4194328
  55.1 0.0 copy-start.8
  55.1 0.0 copy-start
  55.1 0.0 copy-start.4
  55.1 12.1 %shard_map.150 = bf16[320,1024]{1,0:T(8,128)(2,1)} custom-call(bf16[320,1024]{1,0:T(8,128)(2,1)S(1)} %bitcast.13, bf16[1,1024,2048]{2,1,0:T(8,128)(2,1)S(1)} %copy-done.7, bf16[1,1024,2048]{2,1,0:T(8,128)(2,1)} %collective-permute-done.in_b, bf16[1,2048,1024]{2,1,0:T(8,128)(2,1)} %out_a.1, bf16[1,2048,1024]{2,1,0:T(8,128)(2,1)} %collective-permute-done.1.out_b), custom_call_target="tpu_custom_call" | custom-call | flops 5368709120 | bytes 16777216 | tf_op jit(solution)/shard_map/pallas_call | solution.py:178
  67.2 3.5 %all-to-all-start.1 = ((bf16[8,40,1024]{2,1,0:T(8,128)(2,1)}), bf16[8,40,1024]{2,1,0:T(8,128)(2,1)S(1)}, u32[]{:S(2)}, u32[]{:S(2)}) async-start(bf16[8,40,1024]{2,1,0:T(8,128)(2,1)} %bitcast.3), calls=%async_computation.1 | async-start | bytes 1310720 | tf_op jit(solution)/shard_map/all_to_all | solution.py:241
  70.8 0.0 copy-done.8
  70.8 0.1 copy.21.gates
  70.9 41.2 %all-gather.3.cloned.1.call-done = bf16[64,64,1024]{2,1,0:T(8,128)(2,1)} async-done(((bf16[4,64,1024]{2,1,0:T(8,128)(2,1)}), bf16[64,64,1024]{2,1,0:T(8,128)(2,1)}) %all-gather.3.cloned.1.call-update) | async-done | bytes 8388624 | tf_op jit(solution)/shard_map/all_gather | solution.py:225
  112.1 0.0 copy-done
  112.1 0.0 copy-done.4
  112.1 0.0 copy-start.2
  112.1 0.0 copy-start.5
  112.1 0.0 copy-start.6
  112.1 2.5 %shard_map.151 = (bf16[128,1024]{1,0:T(8,128)(2,1)S(1)}, bf16[128,320]{1,0:T(8,128)(2,1)S(1)}, bf16[128,320]{1,0:T(8,128)(2,1)S(1)}) custom-call(bf16[128,1024]{1,0:T(8,128)(2,1)S(1)} %copy-done, f32[1,1024]{1,0:T(1,128)S(1)} %bitcast.15, s32[128,2]{1,0:T(8,128)S(1)} %copy.19.ids, f32[128,2]{1,0:T(8,128)S(1)} %copy.21.gates, bf16[16,4,64,1024]{3,2,1,0:T(8,128)(2,1)} %bitcast.16), custom_call_target="tpu_custom_call" | custom-call | tf_op jit(solution)/shard_map/pallas_call | solution.py:246
  114.6 0.0 all-to-all-done.1
  114.6 0.0 copy-done.2
  114.6 0.0 copy-done.5
  114.6 0.0 copy-done.6
  114.6 6.0 %shard_map.152 = (bf16[128,1024]{1,0:T(8,128)(2,1)}, bf16[128,1024]{1,0:T(8,128)(2,1)}) custom-call(s32[2]{0:T(128)S(1)} %copy-done.5, s32[2]{0:T(128)S(1)} %copy-done.6, bf16[320,1024]{1,0:T(8,128)(2,1)S(1)} %bitcast.12, bf16[128,320]{1,0:T(8,128)(2,1)S(1)} %get-tuple-element.5.high, bf16[128,320]{1,0:T(8,128)(2,1)S(1)} %get-tuple-element.6.low, ...), custom_call_target="tpu_custom_call" | custom-call | tf_op jit(solution)/shard_map/pallas_call | solution.py:261
Async XLA Ops:
  7.2 104.9 %all-gather.3.cloned.1.call-start = ((), (), s32[]{:S(2)}) async-start(), calls=%async_computation.2 | async-start | bytes 8912896 | tf_op jit(solution)/shard_map/all_gather | solution.py:225
  9.2 43.7 %collective-permute-start = (bf16[1,1024,2048]{2,1,0:T(8,128)(2,1)}, bf16[1,1024,2048]{2,1,0:T(8,128)(2,1)}, u32[]{:S(2)}, u32[]{:S(2)}) collective-permute-start(bf16[1,1024,2048]{2,1,0:T(8,128)(2,1)} %in_a.1), channel_id=1, source_target_pairs={{0,1},{1,0},{2,3},{3,2},{4,5},{5,4},{6,7},{7,6},{8,9},{9,8},{10,11... | collective-permute-start | bytes 12582920 | tf_op jit(solution)/shard_map/ppermute | solution.py:193
  9.7 43.2 %collective-permute-start.1 = (bf16[1,2048,1024]{2,1,0:T(8,128)(2,1)}, bf16[1,2048,1024]{2,1,0:T(8,128)(2,1)}, u32[]{:S(2)}, u32[]{:S(2)}) collective-permute-start(bf16[1,2048,1024]{2,1,0:T(8,128)(2,1)} %out_a.1), channel_id=1, source_target_pairs={{0,1},{1,0},{2,3},{3,2},{4,5},{5,4},{6,7},{7,6},{8,9},{9,8},{10,11... | collective-permute-start | bytes 12582920 | tf_op jit(solution)/shard_map/ppermute | solution.py:193
  10.6 0.9 copy-start.1
  11.5 0.7 copy-start.3
  52.9 2.2 %copy-start.7 = (bf16[1,1024,2048]{2,1,0:T(8,128)(2,1)S(1)}, bf16[1,1024,2048]{2,1,0:T(8,128)(2,1)}, u32[]{:S(2)}) copy-start(bf16[1,1024,2048]{2,1,0:T(8,128)(2,1)} %in_a.1) | copy-start | bytes 12582916
  55.1 15.7 %copy-start.8 = (f32[128,2]{0,1:T(2,128)S(1)}, f32[128,2]{0,1:T(2,128)}, u32[]{:S(2)}) copy-start(f32[128,2]{0,1:T(2,128)} %param.17) | copy-start | bytes 3076
  55.1 57.0 %copy-start = (bf16[128,1024]{1,0:T(8,128)(2,1)S(1)}, bf16[128,1024]{1,0:T(8,128)(2,1)}, u32[]{:S(2)}) copy-start(bf16[128,1024]{1,0:T(8,128)(2,1)} %targets.3) | copy-start | bytes 786436
  55.1 57.0 %copy-start.4 = (f32[1024]{0:T(1024)S(1)}, f32[1024]{0:T(1024)}, u32[]{:S(2)}) copy-start(f32[1024]{0:T(1024)} %param.21) | copy-start | bytes 12292
  67.2 47.4 %all-to-all-start.1 = ((bf16[8,40,1024]{2,1,0:T(8,128)(2,1)}), bf16[8,40,1024]{2,1,0:T(8,128)(2,1)S(1)}, u32[]{:S(2)}, u32[]{:S(2)}) async-start(bf16[8,40,1024]{2,1,0:T(8,128)(2,1)} %bitcast.3), calls=%async_computation.1 | async-start | bytes 1310720 | tf_op jit(solution)/shard_map/all_to_all | solution.py:241
  112.1 2.5 %copy-start.2 = (bf16[128,1024]{1,0:T(8,128)(2,1)S(1)}, bf16[128,1024]{1,0:T(8,128)(2,1)}, u32[]{:S(2)}) copy-start(bf16[128,1024]{1,0:T(8,128)(2,1)} %sources.3) | copy-start | bytes 786436
  112.1 2.5 %copy-start.5 = (s32[2]{0:T(128)S(1)}, s32[2]{0:T(128)}, u32[]{:S(2)}) copy-start(s32[2]{0:T(128)} %src_lengths.1) | copy-start | bytes 28
  112.1 2.5 %copy-start.6 = (s32[2]{0:T(128)S(1)}, s32[2]{0:T(128)}, u32[]{:S(2)}) copy-start(s32[2]{0:T(128)} %tgt_lengths.1) | copy-start | bytes 28
Sparse Core Ops, SparseCore 0:
  10.2 101.8 all-gather.2

commit v2 on v1

v2 whole, which is shorter than its diff:
```python
import functools

import jax
import jax.numpy as jnp
from jax import lax
from jax.experimental import pallas as pl
from jax.experimental.pallas import tpu as pltpu
from jax.sharding import Mesh, PartitionSpec as P

DH = 64
F32, BF16 = jnp.float32, jnp.bfloat16
CHIPS = ("hi", "lo")
EXPERT = ("hi", "lo", "pair")
FFN_BLOCK = 1024


def layer_norm(rows, gain):
    rows = rows.astype(F32)
    mean = jnp.mean(rows, axis=-1, keepdims=True)
    centered = rows - mean
    spread = jnp.mean(centered * centered, axis=-1, keepdims=True)
    return centered * lax.rsqrt(spread + 1e-05) * gain


def places(ids, experts, capacity):
    tokens = ids.shape[1]
    count = -(-experts // 16) * 16
    expert = lax.broadcasted_iota(jnp.int32, (count, tokens), 0)
    first, second = (
        jnp.where(expert == ids[j : j + 1, :], 1.0, 0.0).astype(F32) for j in range(2)
    )
    row = lax.broadcasted_iota(jnp.int32, (tokens, tokens), 0)
    col = lax.broadcasted_iota(jnp.int32, (tokens, tokens), 1)
    before = jnp.where(row < col, 1.0, 0.0).astype(BF16)
    earlier = jnp.dot((first + second).astype(BF16), before, preferred_element_type=F32)
    slots = (
        jnp.sum(earlier * first, axis=0, keepdims=True),
        jnp.sum((earlier + first) * second, axis=0, keepdims=True),
    )
    return [ids[j : j + 1, :].astype(F32) * capacity + slots[j] for j in range(2)]


def dispatch(experts, capacity, sources, gain, ids, out):
    tokens = sources.shape[0]
    first, second = places(ids[...], experts, capacity)
    normed = layer_norm(sources[...], gain[...]).astype(BF16)
    slot = lax.broadcasted_iota(jnp.int32, (out.shape[0], tokens), 0).astype(F32)
    pick = jnp.where((slot == first) | (slot == second), 1.0, 0.0).astype(BF16)
    out[...] = jnp.dot(pick, normed, preferred_element_type=F32).astype(BF16)


def prep_kernel(experts, capacity, sources, gain, ids, out):
    dispatch(experts, capacity, sources, gain, ids, out)


def query_kernel(targets, gain, w_q, query):
    tnormed = layer_norm(targets[...], gain[...]).astype(BF16)
    weight = w_q[:, 0].reshape(tnormed.shape[1], -1)
    query[...] = jnp.dot(tnormed, weight, preferred_element_type=F32).astype(BF16)


def combine_matrix(experts, capacity, ids, gates, high, low):
    first, second = places(ids[...], experts, capacity)
    tokens, rows = high.shape
    slot = lax.broadcasted_iota(jnp.int32, (rows, tokens), 0).astype(F32)
    mix = jnp.where(slot == first, gates[0:1, :], 0.0) + jnp.where(slot == second, gates[1:2, :], 0.0)
    mix = jnp.transpose(mix)
    top = mix.astype(BF16)
    high[...] = top
    low[...] = (mix - top.astype(F32)).astype(BF16)


def preload_kernel(experts, capacity, fetched, choices, *refs):
    choice, refs_on = refs[fetched : fetched + choices], refs[fetched + choices :]
    ids, gates = refs_on[:2]
    outs, high, low, sems = refs_on[2:-3], refs_on[-3], refs_on[-2], refs_on[-1]
    copies = [
        pltpu.make_async_copy(refs[i], outs[i], sems.at[i]) for i in range(fetched)
    ]
    for copy in copies:
        copy.start()
    if choices:
        mine = lax.axis_index("pair") == lax.axis_index("groups")
        outs[fetched][...] = jnp.where(mine, choice[0][...], choice[1][...])
    combine_matrix(experts, capacity, ids, gates, high, low)
    for copy in copies:
        copy.wait()


def ffn_kernel(rows, others, w_in, w_out, *rest):
    for source, out in ((others, rest[-1]), (rows, rest[-2])):
        total = None
        block = min(w_in.shape[2], FFN_BLOCK)
        for n in range(0, w_in.shape[2], block):
            hidden = jnp.dot(source[...], w_in[0, :, n : n + block], preferred_element_type=F32)
            hidden = jnp.maximum(hidden, 0.0).astype(BF16)
            term = jnp.dot(hidden, w_out[0, n : n + block, :], preferred_element_type=F32)
            total = term if total is None else total + term
        out[...] = total.astype(BF16)


def memory_of(results, high, low, sources):
    moe = jnp.dot(high, results, preferred_element_type=F32) + jnp.dot(low, results, preferred_element_type=F32)
    return (sources.astype(F32) + moe).astype(BF16)


def attend(query, key, value, lengths, sentences):
    q_rows, k_rows = query.shape[0] // sentences, key.shape[0] // sentences
    both = 2 * DH
    lane = lax.broadcasted_iota(jnp.int32, (query.shape[0], both), 1)
    row = lax.broadcasted_iota(jnp.int32, (query.shape[0], key.shape[0]), 0)
    col = lax.broadcasted_iota(jnp.int32, (query.shape[0], key.shape[0]), 1)
    live = jnp.zeros(row.shape, jnp.bool_)
    for s in range(sentences):
        live = live | (
            (row >= s * q_rows) & (row < (s + 1) * q_rows)
            & (col >= s * k_rows) & (col < s * k_rows + jnp.minimum(lengths[s], k_rows))
        )
    live = jnp.concatenate((live, live), axis=0)
    contexts = []
    for pair in range(query.shape[1] // both):
        columns = slice(pair * both, (pair + 1) * both)
        q = query[:, columns]
        zero = jnp.zeros_like(q)
        q = jnp.concatenate((jnp.where(lane < DH, q, zero), jnp.where(lane < DH, zero, q)), axis=0)
        scores = lax.dot_general(q, key[:, columns], (((1,), (1,)), ((), ())), preferred_element_type=F32)
        scores = jnp.where(live, scores * DH ** (-0.5), -1e30)
        raised = jnp.exp(scores - jnp.max(scores, axis=-1, keepdims=True))
        weights = (raised / jnp.sum(raised, axis=-1, keepdims=True)).astype(BF16)
        mixed = jnp.dot(weights, value[:, columns], preferred_element_type=F32)
        half = query.shape[0]
        contexts.append(jnp.where(lane < DH, mixed[:half], mixed[half:]).astype(BF16))
    return jnp.concatenate(contexts, axis=1)


def tail_kernel(
    sentences, src_lengths, results, high, low, sources, query, gathered, memory, partial_out
):
    mem = memory_of(results[...], high[...], low[...], sources[...])
    memory[...] = mem
    depth = mem.shape[1]
    w_k, w_v, w_o = (gathered[:, i].reshape(depth, -1) for i in (1, 2, 3))
    key = jnp.dot(mem, w_k, preferred_element_type=F32).astype(BF16)
    value = jnp.dot(mem, w_v, preferred_element_type=F32).astype(BF16)
    context = attend(query[...], key, value, src_lengths, sentences)
    partial_out[...] = lax.dot_general(
        context, w_o, (((1,), (1,)), ((), ())), preferred_element_type=F32
    ).astype(partial_out.dtype)


def live_rows(count, lengths, sentences):
    row = lax.broadcasted_iota(jnp.int32, (count, 1), 0)
    each = count // sentences
    live = jnp.zeros((count, 1), jnp.bool_)
    for s in range(sentences):
        live = live | ((row >= s * each) & (row < s * each + jnp.minimum(lengths[s], each)))
    return jnp.where(live, 1.0, 0.0)


def whole(shape, dtype=BF16):
    return jax.ShapeDtypeStruct(shape, dtype)


def full(shape):
    return pl.BlockSpec(shape, lambda i: (0,) * len(shape))


SMEM = pl.BlockSpec(memory_space=pltpu.SMEM)
HERE = pl.BlockSpec(memory_space=pltpu.VMEM)
FAR = pl.BlockSpec(memory_space=pltpu.HBM)
ANY = pl.BlockSpec(memory_space=pl.ANY)
WIDE = pltpu.CompilerParams(vmem_limit_bytes=63 * 2**20)
TIGHT = pltpu.CompilerParams(vmem_limit_bytes=51 * 2**20)
NEAR = pltpu.CompilerParams(vmem_limit_bytes=24 * 2**20)


def estimate(flops, *operands):
    sizes = sum(x.size * x.dtype.itemsize for x in operands)
    return pl.CostEstimate(flops=flops, bytes_accessed=sizes, transcendentals=0)


def call(kernel, out_shape, *operands, specs=None, scratch=(), flops=0):
    specs = specs or {}
    in_specs = [specs.get(i, FAR) for i in range(len(operands))]
    far = [i for i, spec in enumerate(in_specs) if spec is FAR]
    count, single = len(operands), not isinstance(out_shape, tuple)

    def body(*refs):
        ins, rest = list(refs[:count]), refs[count:]
        held, sems = rest[-len(far) - 1 : -1], rest[-1]
        copies = [pltpu.make_async_copy(ins[i], held[n], sems.at[n]) for n, i in enumerate(far)]
        for copy in copies:
            copy.start()
        for copy in copies:
            copy.wait()
        for n, i in enumerate(far):
            ins[i] = held[n]
        kernel(*ins, *rest[: -len(far) - 1])

    moved = [pltpu.VMEM(operands[i].shape, operands[i].dtype) for i in far]
    return pl.pallas_call(
        body,
        grid=(1,),
        in_specs=in_specs,
        out_specs=full(out_shape.shape) if single else [full(o.shape) for o in out_shape],
        out_shape=out_shape,
        scratch_shapes=[*scratch, *moved, pltpu.SemaphoreType.DMA((len(far),))],
        compiler_params=WIDE,
        cost_estimate=estimate(flops, *operands),
    )(*operands)


def near(kernel, out_shape, *operands, tables=0, specs=None, out_specs=None, scratch=(), flops=0, params=None):
    specs = specs or {}
    single = not isinstance(out_shape, tuple)
    return pl.pallas_call(
        kernel,
        in_specs=[specs.get(i, SMEM if i < tables else HERE) for i in range(len(operands))],
        out_specs=out_specs or (HERE if single else [HERE] * len(out_shape)),
        out_shape=out_shape,
        scratch_shapes=list(scratch),
        compiler_params=params or NEAR,
        cost_estimate=estimate(flops, *operands),
    )(*operands)


def ffn(rows, others, w_in, w_out, ahead=()):
    shape = whole((rows.shape[0], w_out.shape[2]))
    return near(
        ffn_kernel,
        (shape, shape), rows, others, w_in, w_out, *ahead,
        specs={4 + i: ANY for i in range(len(ahead))},
        flops=8 * rows.shape[0] * w_in.shape[1] * w_in.shape[2],
    )


def partner(block):
    return lax.ppermute(block, "pair", [(0, 1), (1, 0)])


def prep_pair_kernel(experts, capacity, sources, gain, ids, *rest):
    weights, (out, own, sent) = rest[:-3], rest[-3:]
    core, half = lax.axis_index("pair"), own.shape[2]
    for block, turn in ((own, 1), (sent, 0)):
        for j, weight in enumerate(weights):
            block[j] = jnp.where(core == turn, weight[:, half:], weight[:, :half])
    dispatch(experts, capacity, sources, gain, ids, out)


def assemble(pieces, chips, index, matrix):
    hi, lo, group = (lax.axis_index(name) for name in ("hi", "lo", "groups"))
    for i, piece in enumerate(pieces):
        step, x, y = i // 4, i % 2, i % 4 // 2
        block = piece[index]
        chip = chips[hi, step] + (1 - lo if x else lo)
        start = (chip * 2 + (1 - group if y else group)) * block.shape[0]
        matrix[pl.ds(pl.multiple_of(start, block.shape[0]), block.shape[0]), :] = block


def query_pair_kernel(chips, targets, others, gain, *rest):
    pieces, (query, w_k, w_v, w_o, w_q) = rest[:-5], rest[-5:]
    for index, matrix in enumerate((w_q, w_k, w_v, w_o)):
        assemble(pieces, chips, index, matrix)
    rows = jnp.concatenate((targets[...], others[...]), axis=0)
    tnormed = layer_norm(rows, gain[...]).astype(BF16)
    query[...] = jnp.dot(tnormed, w_q[...], preferred_element_type=F32).astype(BF16)


def combine_kernel(results, high, low, sources, memory, again):
    value = memory_of(results[...], high[...], low[...], sources[...])
    memory[...] = value
    again[...] = value


def tail_pair_kernel(
    sentences, lengths, other_lengths, memory, others, query, w_k, w_v, w_o, kept, sent
):
    mem = jnp.concatenate((memory[...], others[...]), axis=0)
    key = jnp.dot(mem, w_k[...], preferred_element_type=F32).astype(BF16)
    value = jnp.dot(mem, w_v[...], preferred_element_type=F32).astype(BF16)
    count = memory.shape[0]
    t_count = query.shape[0] // 2
    for out, part, live in ((sent, 1, other_lengths), (kept, 0, lengths)):
        rows = slice(part * count, (part + 1) * count)
        context = attend(
            query[part * t_count : (part + 1) * t_count], key[rows], value[rows], live, sentences
        )
        out[...] = lax.dot_general(
            context, w_o[...], (((1,), (1,)), ((), ())), preferred_element_type=F32
        ).astype(out.dtype)


def final_kernel(sentences, tgt_lengths, targets, kept, received, decoded):
    live = live_rows(targets.shape[0], tgt_lengths, sentences)
    total = targets[...].astype(F32) + (kept[...] + received[...].astype(F32))
    decoded[...] = (total * live).astype(BF16)


def ring_order(count):
    return [*range(0, count, 2), *range(count - 1 - count % 2, 0, -2)]


DIAGONAL_BY_X = 2
AHEAD = (1, 2, 3, 4, 5, 6, 8, 12)


def swap(block, axis):
    return lax.ppermute(block, axis, [(0, 1), (1, 0)])


def ring_table(count):
    order = ring_order(count)
    return [
        [order[(order.index(hi) - step) % count] * 2 for step in range(count)] for hi in range(count)
    ]


def gather_pieces(piece):
    count = lax.axis_size("hi")
    order = ring_order(count)
    ring = [(order[i], order[(i + 1) % count]) for i in range(count)]
    pieces = []
    for step in range(count):
        if step:
            piece = lax.ppermute(piece, "hi", ring)
        along_x, along_y = swap(piece, "lo"), swap(piece, "groups")
        diagonal = swap(along_y, "lo") if step == DIAGONAL_BY_X else swap(along_x, "groups")
        pieces += [piece, along_x, along_y, diagonal]
    return pieces


def cross_attention_by_pairs(
    results, high, low, held, others, dec_gain, src_lengths, other_lengths, tgt_lengths, pieces
):
    sources, targets, targets_again = held
    width = sources.shape[1]
    t_tokens = targets.shape[0]
    sentences = src_lengths.shape[0]
    half = pieces[0].shape[2]
    chips = jnp.array(ring_table(lax.axis_size("hi")), jnp.int32)
    matrix = whole((width, half))
    query, w_k, w_v, w_o = near(
        query_pair_kernel,
        (whole((2 * t_tokens, half)), matrix, matrix, matrix),
        chips, targets, others, dec_gain, *pieces,
        tables=1,
        scratch=[pltpu.VMEM((width, half), BF16)],
    )
    memory, again = near(
        combine_kernel, (whole(sources.shape),) * 2, results, high, low, sources
    )
    kept, sent = near(
        functools.partial(tail_pair_kernel, sentences),
        (whole(targets.shape, F32), whole(targets.shape)),
        src_lengths, other_lengths, again, partner(memory), query, w_k, w_v, w_o,
        tables=2,
    )
    decoded = near(
        functools.partial(final_kernel, sentences),
        whole(targets.shape),
        tgt_lengths, targets_again, kept, partner(sent),
        tables=1,
    )
    return memory, decoded


def shards(
    sources,
    enc_gain,
    route_ids,
    route_gates,
    w_in,
    w_out,
    targets,
    dec_gain,
    src_lengths,
    tgt_lengths,
    w_query,
    w_key,
    w_value,
    w_attn,
):
    tokens, width = sources.shape
    experts = lax.axis_size("hi") * lax.axis_size("lo")
    heads = lax.axis_size("head")
    capacity = 2 * ((5 * tokens + 4 * experts - 1) // (4 * experts))
    sentences = src_lengths.shape[0]
    enc_gain, dec_gain = enc_gain.reshape(1, -1), dec_gain.reshape(1, -1)

    ids, gates = route_ids.T, route_gates.T
    by_pairs = heads == 1 and lax.axis_size("groups") == 2 and lax.axis_size("lo") == 2
    prep_args = (sources, enc_gain, ids)
    buffer = whole((experts * capacity, width))
    if by_pairs:
        shape = whole((4, w_query.shape[0], w_query.shape[1] // 2))
        outgoing, own, sent = call(
            functools.partial(prep_pair_kernel, experts, capacity),
            (buffer, shape, shape), *prep_args, w_query, w_key, w_value, w_attn,
        )
        choice = (own, partner(sent))
    else:
        outgoing = call(functools.partial(prep_kernel, experts, capacity), buffer, *prep_args)
        ahead, choice = (), ()
        stacked = jnp.stack((w_query, w_key, w_value, w_attn))
        gathered = lax.all_gather(stacked, EXPERT, axis=0, tiled=False)
    fetched = (w_in, w_out, sources, targets, targets)
    matrix = whole((tokens, experts * capacity))
    w_in, w_out, *held, high, low = near(
        functools.partial(preload_kernel, experts, capacity, len(fetched), len(choice)),
        (*(whole(x.shape) for x in fetched), *(whole(x.shape) for x in choice[:1]), matrix, matrix),
        *fetched, *choice, ids, gates,
        specs={i: FAR for i in range(len(fetched))},
        scratch=[pltpu.SemaphoreType.DMA((len(fetched),))],
        params=TIGHT,
    )
    if by_pairs:
        *held, piece = held
        pieces = gather_pieces(piece)
        others, other_lengths = partner(targets), partner(src_lengths)
        ahead = [pieces[i] for i in AHEAD] + [others, other_lengths]
    arrived = lax.all_to_all(
        outgoing.reshape(experts, capacity, width), CHIPS, split_axis=0, concat_axis=0, tiled=True
    ).reshape(-1, width)
    mine, theirs = ffn(arrived, partner(arrived), w_in, w_out, ahead)
    if heads > 1:
        mine, theirs = (lax.psum(x.astype(F32), "head").astype(BF16) for x in (mine, theirs))
    half = (mine.astype(F32) + partner(theirs).astype(F32)).astype(BF16)
    results = lax.all_to_all(
        half.reshape(experts, capacity, width), CHIPS, split_axis=0, concat_axis=0, tiled=True
    ).reshape(-1, width)

    if by_pairs:
        return cross_attention_by_pairs(
            results, high, low, held, others, dec_gain, src_lengths, other_lengths, tgt_lengths, pieces
        )
    query = call(query_kernel, whole((targets.shape[0], w_query.shape[1])), targets, dec_gain, gathered)
    memory, partial_out = call(
        functools.partial(tail_kernel, sentences),
        (whole(sources.shape), whole(targets.shape)),
        src_lengths, results, high, low, sources, query, gathered,
        specs={0: SMEM},
    )
    attn = lax.psum_scatter(partial_out, "head", scatter_dimension=1, tiled=True).astype(F32)
    share = width // heads
    own = lax.dynamic_slice_in_dim(targets, lax.axis_index("head") * share, share, 1).astype(F32)
    each = targets.shape[0] // sentences
    positions = jnp.arange(targets.shape[0], dtype=jnp.int32)
    live = (positions % each < jnp.take(tgt_lengths, positions // each)).astype(F32)
    return memory, ((own + attn) * live[:, None]).astype(BF16)


def solution(mesh):
    groups, experts, heads = (mesh.shape[name] for name in ("groups", "expert", "head"))
    chips = experts // 2
    low = 2 if chips % 2 == 0 else 1
    fine = Mesh(
        mesh.devices.reshape(groups, chips // low, low, 2, heads),
        ("groups", "hi", "lo", "pair", "head"),
    )
    rows = ("groups", "hi", "lo", "pair")
    placed = (
        P(rows, None),
        P(),
        P(rows, None),
        P(rows, None),
        P(EXPERT, None, "head"),
        P(EXPERT, "head", None),
        P(rows, None),
        P(),
        P(rows),
        P(rows),
        P(EXPERT, "head"),
        P(EXPERT, "head"),
        P(EXPERT, "head"),
        P(EXPERT, "head"),
    )
    return jax.shard_map(
        shards,
        mesh=fine,
        in_specs=placed,
        out_specs=(P(rows, None), P(rows, "head")),
        check_vma=False,
    )
```

time: 128 us -> 106 us (0.83)
  blocking collectives: 39.8 us -> 0 us
  starting transfers between devices: 4.18 us -> 37.4 us
  between operations: 14.1 us -> 0.82 us
  waiting for transfers between devices: 41.2 us -> 29.5 us
  local copies, waits for them, and re-layouts: 4.74 us -> 13.8 us
  Pallas kernels: 21.4 us -> 22.9 us
    all_gather x1 -> x0, waiting for transfers between devices: 41.2 us -> none  [shards(): gathered = lax.all_gather(stacked, EXPERT, axis=0, tiled=False)]
    all_to_all x1 -> x0, blocking collectives: 39.8 us -> none  [shards(): lax.all_to_all(outgoing.reshape(experts, capacity, width), CHIPS, split_a...]
    ppermute x0 -> x15, starting transfers between devices: none -> 25.4 us  [the longest x12 15.8 us: swap(): return lax.ppermute(block, axis, [(0, 1), (1, 0)])]
    ppermute x0 -> x15, waiting for transfers between devices: none -> 23.4 us  [the longest x12 20.3 us: swap(): return lax.ppermute(block, axis, [(0, 1), (1, 0)])]
    unnamed x20 -> x44, local copies, waits for them, and re-layouts: 4.74 us -> 13.8 us
    all_to_all x0 -> x1, starting transfers between devices: none -> 7.26 us  [shards(): lax.all_to_all(outgoing.reshape(experts, capacity, width), CHIPS, split_a...]
    ppermute x2 -> x7, waiting for transfers between devices: 0.01 us -> 5.79 us  [partner(): return lax.ppermute(block, 'pair', [(0, 1), (1, 0)])]
    another operation x1 -> x0, other arithmetic: 1.97 us -> none  [shards(): stacked = jnp.stack((w_query, w_key, w_value, w_attn))]
  transfers between devices with their start and end apart: 4 -> 24, of which waited for: 1 -> 13; matrix products, arithmetic and copies ran while one was open for 1% -> 0% of each run, Pallas kernels for 12% -> 10%
where the time goes in v2:
time: 106 us; the launch traced here: 105 us
  starting transfers between devices  37.4 us (35%)
  waiting for transfers between devices  29.5 us (28%)
  Pallas kernels  22.9 us (22%)
  local copies, waits for them, and re-layouts  13.8 us (13%)
  other arithmetic  1.1 us (1%)
    ppermute x12, waiting for transfers between devices, swap(): return lax.ppermute(block, axis, [(0, 1), (1, 0)])  20.3 us
    pallas_call x6, Pallas kernels, near(): pl.pallas_call(kernel, in_specs=[specs.get(i, SMEM if i < tables else HER...  20.1 us
    ppermute x12, starting transfers between devices, swap(): return lax.ppermute(block, axis, [(0, 1), (1, 0)])  15.8 us
    unnamed x44, local copies, waits for them, and re-layouts  13.8 us
    ppermute x3, starting transfers between devices, gather_pieces(): piece = lax.ppermute(piece, 'hi', ring)  9.66 us
    all_to_all x1, starting transfers between devices, shards(): lax.all_to_all(outgoing.reshape(experts, capacity, width), CHIPS, split_a...  7.26 us
    ppermute x7, waiting for transfers between devices, partner(): return lax.ppermute(block, 'pair', [(0, 1), (1, 0)])  5.79 us
    all_to_all x1, starting transfers between devices, shards(): lax.all_to_all(half.reshape(experts, capacity, width), CHIPS, split_axis=...  3.94 us
  transfers between devices with their start and end apart: 24, of which 13 were waited for; matrix products, arithmetic and copies ran while one was open for 0% of the time, Pallas kernels for 10%

profile of v2, /device:TPU:0, one launch (start us, length us, event | category | flops | bytes accessed | tf_op | source)
XLA Modules:
  0.0 105.4 jit_solution(14691443516340256098)
XLA Ops:
  0.6 2.8 %shard_map.158 = (bf16[320,1024]{1,0:T(8,128)(2,1)}, bf16[4,64,512]{2,1,0:T(8,128)(2,1)}, bf16[4,64,512]{2,1,0:T(8,128)(2,1)}) custom-call(bf16[128,1024]{1,0:T(8,128)(2,1)} %refs_2_.1, f32[1,1024]{1,0:T(1,128)} %bitcast.17, s32[2,128]{1,0:T(2,128)} %bitcast.12, bf16[64,1024]{1,0:T(8,128)(2,1)} %refs_3_.2, bf16[64,1024]{1,0:T(8,128)(2,1)} %refs_4_.2, ...), custom_call_target="tpu_custom_call" | custom-call | bytes 791552 | tf_op jit(solution)/shard_map/pallas_call | solution.py:201
  3.4 7.3 %all-to-all-start = ((bf16[8,40,1024]{2,1,0:T(8,128)(2,1)}), bf16[8,40,1024]{2,1,0:T(8,128)(2,1)S(1)}, u32[]{:S(2)}, u32[]{:S(2)}) async-start(bf16[8,40,1024]{2,1,0:T(8,128)(2,1)} %bitcast.16), calls=%async_computation | async-start | bytes 1310720 | tf_op jit(solution)/shard_map/all_to_all | solution.py:421
  10.7 0.0 collective-permute-start.1
  10.7 1.7 %collective-permute-done.1.refs_6_ = bf16[4,64,512]{2,1,0:T(8,128)(2,1)S(1)} collective-permute-done((bf16[4,64,512]{2,1,0:T(8,128)(2,1)}, bf16[4,64,512]{2,1,0:T(8,128)(2,1)S(1)}, u32[]{:S(2)}, u32[]{:S(2)}) %collective-permute-start.1) | collective-permute-done | bytes 262176 | tf_op jit(solution)/shard_map/ppermute | solution.py:238
  12.4 0.9 copy-done
  13.4 0.9 copy-done.1
  14.3 0.9 copy-done.9
  15.3 0.7 copy-done.15
  15.9 0.7 copy-done.17
  16.6 6.9 %shard_map.159 = (bf16[1,1024,2048]{2,1,0:T(8,128)(2,1)}, bf16[1,2048,1024]{2,1,0:T(8,128)(2,1)}, bf16[128,1024]{1,0:T(8,128)(2,1)S(1)}, bf16[128,1024]{1,0:T(8,...) custom-call(bf16[1,1024,2048]{2,1,0:T(8,128)(2,1)} %refs_0_.3, ...), custom_call_target="tpu_custom_call" | custom-call | bytes 9701376 | tf_op jit(solution)/shard_map/pallas_call | solution.py:216
  23.5 0.0 copy-start.10
  23.5 0.6 copy-done.10
  24.1 0.6 copy-done.12
  24.8 2.9 %collective-permute-start.5 = (bf16[4,64,512]{2,1,0:T(8,128)(2,1)S(1)}, bf16[4,64,512]{2,1,0:T(8,128)(2,1)S(1)}, u32[]{:S(2)}, u32[]{:S(2)}) collective-permute-start(bf16[4,64,512]{2,1,0:T(8,128)(2,1)S(1)} %get-tuple-element.28.rest_0_), channel_id=1, source_target_pairs={{0,8},{8,12},{12,4},{4,0},{1,9},{9,13},{13,5},{5,1},{2,10},{10,14}... | collective-permute-start | bytes 786440 | tf_op jit(solution)/shard_map/ppermute | solution.py:325
  27.7 0.3 all-to-all-done
  28.0 0.5 collective-permute-start.10
  28.5 0.1 collective-permute-start.11
  28.6 1.4 %collective-permute-start.2 = (bf16[4,64,512]{2,1,0:T(8,128)(2,1)S(1)}, bf16[4,64,512]{2,1,0:T(8,128)(2,1)S(1)}, u32[]{:S(2)}, u32[]{:S(2)}) collective-permute-start(bf16[4,64,512]{2,1,0:T(8,128)(2,1)S(1)} %get-tuple-element.28.rest_0_), channel_id=1, source_target_pairs={{0,2},{2,0},{1,3},{3,1},{4,6},{6,4},{5,7},{7,5},{8,10},{10,8},{9,1... | collective-permute-start | bytes 786440 | tf_op jit(solution)/shard_map/ppermute | solution.py:308
  30.0 0.4 collective-permute-done.11.rest_9_.other_lengths
  30.5 1.5 %collective-permute-start.3 = (bf16[4,64,512]{2,1,0:T(8,128)(2,1)S(1)}, bf16[4,64,512]{2,1,0:T(8,128)(2,1)S(1)}, u32[]{:S(2)}, u32[]{:S(2)}) collective-permute-start(bf16[4,64,512]{2,1,0:T(8,128)(2,1)S(1)} %get-tuple-element.28.rest_0_), channel_id=1, source_target_pairs={{0,16},{16,0},{1,17},{17,1},{2,18},{18,2},{3,19},{19,3},{4,20},{20... | collective-permute-start | bytes 786440 | tf_op jit(solution)/shard_map/ppermute | solution.py:308
  32.0 1.6 %collective-permute-done.5.rest_3_.rest_4_ = bf16[4,64,512]{2,1,0:T(8,128)(2,1)S(1)} collective-permute-done((bf16[4,64,512]{2,1,0:T(8,128)(2,1)S(1)}, bf16[4,64,512]{2,1,0:T(8,128)(2,1)S(1)}, u32[]{:S(2)}, u32[]{:S(2)}) %collective-permute-start.5) | collective-permute-done | bytes 262176 | tf_op jit(solution)/shard_map/ppermute | solution.py:325
  33.6 3.4 %collective-permute-start.8 = (bf16[4,64,512]{2,1,0:T(8,128)(2,1)S(1)}, bf16[4,64,512]{2,1,0:T(8,128)(2,1)S(1)}, u32[]{:S(2)}, u32[]{:S(2)}) collective-permute-start(bf16[4,64,512]{2,1,0:T(8,128)(2,1)S(1)} %collective-permute-done.5.rest_3_.rest_4_), channel_id=1, source_target_pairs={{0,8},{8,12},{12,4},{4,0},{1,9},{9,13},{13,5},{5,1},{2,10},{10,14}... | collective-permute-start | bytes 786440 | tf_op jit(solution)/shard_map/ppermute | solution.py:325
  36.9 0.0 collective-permute-done.10.rest_8_.others
  36.9 1.5 %collective-permute-start.6 = (bf16[4,64,512]{2,1,0:T(8,128)(2,1)S(1)}, bf16[4,64,512]{2,1,0:T(8,128)(2,1)S(1)}, u32[]{:S(2)}, u32[]{:S(2)}) collective-permute-start(bf16[4,64,512]{2,1,0:T(8,128)(2,1)S(1)} %collective-permute-done.5.rest_3_.rest_4_), channel_id=1, source_target_pairs={{0,2},{2,0},{1,3},{3,1},{4,6},{6,4},{5,7},{7,5},{8,10},{10,8},{9,1... | collective-permute-start | bytes 786440 | tf_op jit(solution)/shard_map/ppermute | solution.py:308
  38.4 1.5 %collective-permute-start.4 = (bf16[4,64,512]{2,1,0:T(8,128)(2,1)S(1)}, bf16[4,64,512]{2,1,0:T(8,128)(2,1)S(1)}, u32[]{:S(2)}, u32[]{:S(2)}) collective-permute-start(bf16[4,64,512]{2,1,0:T(8,128)(2,1)S(1)} %collective-permute-done.2.rest_0_.rest_1_), channel_id=1, source_target_pairs={{0,16},{16,0},{1,17},{17,1},{2,18},{18,2},{3,19},{19,3},{4,20},{20... | collective-permute-start | bytes 786440 | tf_op jit(solution)/shard_map/ppermute | solution.py:308
  39.9 0.0 collective-permute-done.3.rest_1_.rest_2_
  39.9 0.5 collective-permute-start.7
  40.4 1.5 %collective-permute-done.8.rest_6_.rest_8_ = bf16[4,64,512]{2,1,0:T(8,128)(2,1)S(1)} collective-permute-done((bf16[4,64,512]{2,1,0:T(8,128)(2,1)S(1)}, bf16[4,64,512]{2,1,0:T(8,128)(2,1)S(1)}, u32[]{:S(2)}, u32[]{:S(2)}) %collective-permute-start.8) | collective-permute-done | bytes 262176 | tf_op jit(solution)/shard_map/ppermute | solution.py:325
  42.0 3.4 %collective-permute-start.9 = (bf16[4,64,512]{2,1,0:T(8,128)(2,1)S(1)}, bf16[4,64,512]{2,1,0:T(8,128)(2,1)S(1)}, u32[]{:S(2)}, u32[]{:S(2)}) collective-permute-start(bf16[4,64,512]{2,1,0:T(8,128)(2,1)S(1)} %collective-permute-done.8.rest_6_.rest_8_), channel_id=1, source_target_pairs={{0,8},{8,12},{12,4},{4,0},{1,9},{9,13},{13,5},{5,1},{2,10},{10,14}... | collective-permute-start | bytes 786440 | tf_op jit(solution)/shard_map/ppermute | solution.py:325
  45.4 2.3 %collective-permute-done.4.rest_2_.rest_3_ = bf16[4,64,512]{2,1,0:T(8,128)(2,1)S(1)} collective-permute-done((bf16[4,64,512]{2,1,0:T(8,128)(2,1)S(1)}, bf16[4,64,512]{2,1,0:T(8,128)(2,1)S(1)}, u32[]{:S(2)}, u32[]{:S(2)}) %collective-permute-start.4) | collective-permute-done | bytes 262176 | tf_op jit(solution)/shard_map/ppermute | solution.py:308
  47.7 0.0 collective-permute-done.6.rest_4_.rest_5_
  47.7 3.3 %collective-permute-done.7.rest_5_.rest_6_ = bf16[4,64,512]{2,1,0:T(8,128)(2,1)S(1)} collective-permute-done((bf16[4,64,512]{2,1,0:T(8,128)(2,1)S(1)}, bf16[4,64,512]{2,1,0:T(8,128)(2,1)S(1)}, u32[]{:S(2)}, u32[]{:S(2)}) %collective-permute-start.7) | collective-permute-done | bytes 262176 | tf_op jit(solution)/shard_map/ppermute | solution.py:308
  51.0 0.0 collective-permute-done.9.rest_7_.rest_12_
  51.0 2.4 %copy-done.20 = bf16[1,1024,2048]{2,1,0:T(8,128)(2,1)S(1)} copy-done((bf16[1,1024,2048]{2,1,0:T(8,128)(2,1)S(1)}, bf16[1,1024,2048]{2,1,0:T(8,128)(2,1)}, u32[]{:S(2)}) %copy-start.20) | copy-done | bytes 4194328
  53.4 2.2 %copy-done.21 = bf16[1,2048,1024]{2,1,0:T(8,128)(2,1)S(1)} copy-done((bf16[1,2048,1024]{2,1,0:T(8,128)(2,1)S(1)}, bf16[1,2048,1024]{2,1,0:T(8,128)(2,1)}, u32[]{:S(2)}) %copy-start.21) | copy-done | bytes 4194328
  55.6 5.6 %shard_map.160 = (bf16[320,1024]{1,0:T(8,128)(2,1)S(1)}, bf16[320,1024]{1,0:T(8,128)(2,1)S(1)}) custom-call(bf16[320,1024]{1,0:T(8,128)(2,1)S(1)} %bitcast.10, bf16[320,1024]{1,0:T(8,128)(2,1)S(1)} %collective-permute-done.others, bf16[1,1024,2048]{2,1,0:T(8,128)(2,1)S(1)} %copy-done.20, bf16[1,2048,1024]{2,1,0:T(8,128)(2,1)S(1)} %copy-done.21, ...), custom_call_target="tpu_custom_call" | custom-call | flops 5368709120 | bytes 12058632 | tf_op jit(solution)/shard_map/pallas_call | solution.py:216
  61.2 0.0 copy-start.14
  61.2 0.0 copy-start.16
  61.2 0.0 copy-start.4
  61.2 0.1 collective-permute-start.12
  61.3 2.1 %collective-permute-done.12 = bf16[320,1024]{1,0:T(8,128)(2,1)S(1)} collective-permute-done((bf16[320,1024]{1,0:T(8,128)(2,1)S(1)}, bf16[320,1024]{1,0:T(8,128)(2,1)S(1)}, u32[]{:S(2)}, u32[]{:S(2)}) %collective-permute-start.12) | collective-permute-done | bytes 655392 | tf_op jit(solution)/shard_map/ppermute | solution.py:238
  63.4 1.1 %add_convert_fusion = bf16[320,1024]{1,0:T(8,128)(2,1)} fusion(bf16[320,1024]{1,0:T(8,128)(2,1)S(1)} %collective-permute-done.12, bf16[320,1024]{1,0:T(8,128)(2,1)S(1)} %get-tuple-element.29), kind=kLoop, calls=%fused_computation | loop fusion | flops 1310720 | bytes 1966080 | tf_op jit(solution)/shard_map/convert_element_type | solution.py:427
  64.5 3.9 %all-to-all-start.1 = ((bf16[8,40,1024]{2,1,0:T(8,128)(2,1)}), bf16[8,40,1024]{2,1,0:T(8,128)(2,1)S(1)}, u32[]{:S(2)}, u32[]{:S(2)}) async-start(bf16[8,40,1024]{2,1,0:T(8,128)(2,1)} %bitcast.15), calls=%async_computation.1 | async-start | bytes 1310720 | tf_op jit(solution)/shard_map/all_to_all | solution.py:428
  68.4 1.5 %collective-permute-start.16 = (bf16[4,64,512]{2,1,0:T(8,128)(2,1)S(1)}, bf16[4,64,512]{2,1,0:T(8,128)(2,1)}, u32[]{:S(2)}, u32[]{:S(2)}) collective-permute-start(bf16[4,64,512]{2,1,0:T(8,128)(2,1)S(1)} %collective-permute-done.8.rest_6_.rest_8_), channel_id=1, source_target_pairs={{0,16},{16,0},{1,17},{17,1},{2,18},{18,2},{3,19},{19,3},{4,20},{20... | collective-permute-start | bytes 786440 | tf_op jit(solution)/shard_map/ppermute | solution.py:308
  69.9 2.0 %collective-permute-start.18 = (bf16[4,64,512]{2,1,0:T(8,128)(2,1)}, bf16[4,64,512]{2,1,0:T(8,128)(2,1)}, u32[]{:S(2)}, u32[]{:S(2)}) collective-permute-start(bf16[4,64,512]{2,1,0:T(8,128)(2,1)} %copy-done.7), channel_id=1, source_target_pairs={{0,2},{2,0},{1,3},{3,1},{4,6},{6,4},{5,7},{7,5},{8,10},{10,8},{9,1... | collective-permute-start | bytes 786440 | tf_op jit(solution)/shard_map/ppermute | solution.py:308
  72.0 0.5 collective-permute-start.14
  72.5 0.0 collective-permute-start.15
  72.5 1.5 %collective-permute-start.19 = (bf16[4,64,512]{2,1,0:T(8,128)(2,1)}, bf16[4,64,512]{2,1,0:T(8,128)(2,1)}, u32[]{:S(2)}, u32[]{:S(2)}) collective-permute-start(bf16[4,64,512]{2,1,0:T(8,128)(2,1)} %copy-done.7), channel_id=1, source_target_pairs={{0,16},{16,0},{1,17},{17,1},{2,18},{18,2},{3,19},{19,3},{4,20},{20... | collective-permute-start | bytes 786440 | tf_op jit(solution)/shard_map/ppermute | solution.py:308
  74.0 3.7 %collective-permute-done.16.rest_10_ = bf16[4,64,512]{2,1,0:T(8,128)(2,1)} collective-permute-done((bf16[4,64,512]{2,1,0:T(8,128)(2,1)S(1)}, bf16[4,64,512]{2,1,0:T(8,128)(2,1)}, u32[]{:S(2)}, u32[]{:S(2)}) %collective-permute-start.16) | collective-permute-done | bytes 262176 | tf_op jit(solution)/shard_map/ppermute | solution.py:308
  77.7 2.1 %collective-permute-start.17 = (bf16[4,64,512]{2,1,0:T(8,128)(2,1)}, bf16[4,64,512]{2,1,0:T(8,128)(2,1)}, u32[]{:S(2)}, u32[]{:S(2)}) collective-permute-start(bf16[4,64,512]{2,1,0:T(8,128)(2,1)} %collective-permute-done.16.rest_10_), channel_id=1, source_target_pairs={{0,2},{2,0},{1,3},{3,1},{4,6},{6,4},{5,7},{7,5},{8,10},{10,8},{9,1... | collective-permute-start | bytes 786440 | tf_op jit(solution)/shard_map/ppermute | solution.py:308
  79.8 5.0 %collective-permute-done.18.rest_13_ = bf16[4,64,512]{2,1,0:T(8,128)(2,1)} collective-permute-done((bf16[4,64,512]{2,1,0:T(8,128)(2,1)}, bf16[4,64,512]{2,1,0:T(8,128)(2,1)}, u32[]{:S(2)}, u32[]{:S(2)}) %collective-permute-start.18) | collective-permute-done | bytes 262176 | tf_op jit(solution)/shard_map/ppermute | solution.py:308
  84.8 1.7 %collective-permute-start.20 = (bf16[4,64,512]{2,1,0:T(8,128)(2,1)}, bf16[4,64,512]{2,1,0:T(8,128)(2,1)}, u32[]{:S(2)}, u32[]{:S(2)}) collective-permute-start(bf16[4,64,512]{2,1,0:T(8,128)(2,1)} %collective-permute-done.18.rest_13_), channel_id=1, source_target_pairs={{0,16},{16,0},{1,17},{17,1},{2,18},{18,2},{3,19},{19,3},{4,20},{20... | collective-permute-start | bytes 786440 | tf_op jit(solution)/shard_map/ppermute | solution.py:308
  86.5 0.9 copy-done.11
  87.4 0.9 copy-done.13
  88.3 1.1 %shard_map.161 = (bf16[128,1024]{1,0:T(8,128)(2,1)}, bf16[128,1024]{1,0:T(8,128)(2,1)S(1)}) custom-call(bf16[320,1024]{1,0:T(8,128)(2,1)S(1)} %bitcast.8, bf16[128,320]{1,0:T(8,128)(2,1)S(1)} %copy-done.11, bf16[128,320]{1,0:T(8,128)(2,1)S(1)} %copy-done.13, bf16[128,1024]{1,0:T(8,128)(2,1)S(1)} %get-tuple-element.33.sources), custom_call_target="tpu_custom_call" | custom-call | bytes 1081344 | tf_op jit(solution)/shard_map/pallas_call | solution.py:216
  89.4 1.0 collective-permute-done.15.rest_9_
  90.4 4.9 %collective-permute-done.17.rest_11_ = bf16[4,64,512]{2,1,0:T(8,128)(2,1)} collective-permute-done((bf16[4,64,512]{2,1,0:T(8,128)(2,1)}, bf16[4,64,512]{2,1,0:T(8,128)(2,1)}, u32[]{:S(2)}, u32[]{:S(2)}) %collective-permute-start.17) | collective-permute-done | bytes 262176 | tf_op jit(solution)/shard_map/ppermute | solution.py:308
  95.3 0.9 copy-done.6
  96.3 0.9 copy-done.8
  97.2 2.3 %shard_map.162 = (bf16[256,512]{1,0:T(8,128)(2,1)S(1)}, bf16[1024,512]{1,0:T(8,128)(2,1)S(1)}, bf16[1024,512]{1,0:T(8,128)(2,1)S(1)}, bf16[1024,512]{1,0:T(8,128)(2,1)S(1)}) custom-call(s32[4,4]{1,0:T(4,128)S(1)} %copy-done.16, bf16[128,1024]{1,0:T(8,128)(2,1)S(1)} %get-tuple-element.37.targets, ...), custom_call_target="tpu_custom_call" | custom-call | bytes 4722752 | tf_op jit(solution)/shard_map/pallas_call | solution.py:216
  99.6 2.9 %shard_map.163 = (f32[128,1024]{1,0:T(8,128)S(1)}, bf16[128,1024]{1,0:T(8,128)(2,1)S(1)}) custom-call(s32[2]{0:T(128)S(1)} %copy-done.18, s32[2]{0:T(128)S(1)} %collective-permute-done.11.rest_9_.other_lengths, bf16[128,1024]{1,0:T(8,128)(2,1)S(1)} %get-tuple-element.36.memory, bf16[128,1024]{1,0:T(8,128)(2,1)S(1)} %collective-permute-done.13.others, ...), custom_call_target="tpu_custom_call" | custom-call | bytes 3932176 | tf_op jit(solution)/shard_map/pallas_call | solution.py:216
  102.4 0.1 collective-permute-start.21
  102.5 1.5 %collective-permute-done.21.received = bf16[128,1024]{1,0:T(8,128)(2,1)S(1)} collective-permute-done((bf16[128,1024]{1,0:T(8,128)(2,1)S(1)}, bf16[128,1024]{1,0:T(8,128)(2,1)S(1)}, u32[]{:S(2)}, u32[]{:S(2)}) %collective-permute-start.21) | collective-permute-done | bytes 262176 | tf_op jit(solution)/shard_map/ppermute | solution.py:238
  104.1 1.4 %shard_map.164 = bf16[128,1024]{1,0:T(8,128)(2,1)} custom-call(s32[2]{0:T(128)S(1)} %copy-done.19, bf16[128,1024]{1,0:T(8,128)(2,1)S(1)} %get-tuple-element.35.targets, f32[128,1024]{1,0:T(8,128)S(1)} %get-tuple-element.42.kept, bf16[128,1024]{1,0:T(8,128)(2,1)S(1)} %collective-permute-done.21.received), custom_call_target="tpu_custom_call" | custom-call | bytes 1048584 | tf_op jit(solution)/shard_map/pallas_call | solution.py:216
  (36 shorter events, 0.1 us)
Async XLA Ops:
  3.4 24.6 %all-to-all-start = ((bf16[8,40,1024]{2,1,0:T(8,128)(2,1)}), bf16[8,40,1024]{2,1,0:T(8,128)(2,1)S(1)}, u32[]{:S(2)}, u32[]{:S(2)}) async-start(bf16[8,40,1024]{2,1,0:T(8,128)(2,1)} %bitcast.16), calls=%async_computation | async-start | bytes 1310720 | tf_op jit(solution)/shard_map/all_to_all | solution.py:421
  10.7 1.7 %collective-permute-start.1 = (bf16[4,64,512]{2,1,0:T(8,128)(2,1)}, bf16[4,64,512]{2,1,0:T(8,128)(2,1)S(1)}, u32[]{:S(2)}, u32[]{:S(2)}) collective-permute-start(bf16[4,64,512]{2,1,0:T(8,128)(2,1)} %get-tuple-element.25), channel_id=1, source_target_pairs={{0,1},{1,0},{2,3},{3,2},{4,5},{5,4},{6,7},{7,6},{8,9},{9,8},{10,11... | collective-permute-start | bytes 786440 | tf_op jit(solution)/shard_map/ppermute | solution.py:238
  12.4 1.0 copy-start
  13.4 0.9 copy-start.1
  14.3 0.9 copy-start.9
  15.3 0.7 copy-start.15
  15.9 0.7 copy-start.17
  16.6 11.4 %copy-start.2 = (bf16[128,1024]{1,0:T(8,128)(2,1)S(1)}, bf16[128,1024]{1,0:T(8,128)(2,1)}, u32[]{:S(2)}) copy-start(bf16[128,1024]{1,0:T(8,128)(2,1)} %refs_4_.3) | copy-start | bytes 786436
  16.6 11.9 %copy-start.18 = (s32[2]{0:T(128)S(1)}, s32[2]{0:T(128)}, u32[]{:S(2)}) copy-start(s32[2]{0:T(128)} %lengths.1) | copy-start | bytes 28
  23.5 0.6 copy-start.10
  24.1 0.6 copy-start.12
  24.8 8.8 %collective-permute-start.5 = (bf16[4,64,512]{2,1,0:T(8,128)(2,1)S(1)}, bf16[4,64,512]{2,1,0:T(8,128)(2,1)S(1)}, u32[]{:S(2)}, u32[]{:S(2)}) collective-permute-start(bf16[4,64,512]{2,1,0:T(8,128)(2,1)S(1)} %get-tuple-element.28.rest_0_), channel_id=1, source_target_pairs={{0,8},{8,12},{12,4},{4,0},{1,9},{9,13},{13,5},{5,1},{2,10},{10,14}... | collective-permute-start | bytes 786440 | tf_op jit(solution)/shard_map/ppermute | solution.py:325
  28.0 23.0 %collective-permute-start = (bf16[320,1024]{1,0:T(8,128)(2,1)S(1)}, bf16[320,1024]{1,0:T(8,128)(2,1)S(1)}, u32[]{:S(2)}, u32[]{:S(2)}) collective-permute-start(bf16[320,1024]{1,0:T(8,128)(2,1)S(1)} %bitcast.9), channel_id=1, source_target_pairs={{0,1},{1,0},{2,3},{3,2},{4,5},{5,4},{6,7},{7,6},{8,9},{9,8},{10,11... | collective-permute-start | bytes 1966088 | tf_op jit(solution)/shard_map/ppermute | solution.py:238
  28.0 9.0 %collective-permute-start.10 = (bf16[128,1024]{1,0:T(8,128)(2,1)S(1)}, bf16[128,1024]{1,0:T(8,128)(2,1)S(1)}, u32[]{:S(2)}, u32[]{:S(2)}) collective-permute-start(bf16[128,1024]{1,0:T(8,128)(2,1)S(1)} %copy-done.2), channel_id=1, source_target_pairs={{0,1},{1,0},{2,3},{3,2},{4,5},{5,4},{6,7},{7,6},{8,9},{9,8},{10,11... | collective-permute-start | bytes 786440 | tf_op jit(solution)/shard_map/ppermute | solution.py:238
  28.5 2.0 %collective-permute-start.11 = (s32[2]{0:T(128)S(1)}, s32[2]{0:T(128)S(1)}, u32[]{:S(2)}, u32[]{:S(2)}) collective-permute-start(s32[2]{0:T(128)S(1)} %copy-done.18), channel_id=1, source_target_pairs={{0,1},{1,0},{2,3},{3,2},{4,5},{5,4},{6,7},{7,6},{8,9},{9,8},{10,11... | collective-permute-start | bytes 32 | tf_op jit(solution)/shard_map/ppermute | solution.py:238
  28.6 9.8 %collective-permute-start.2 = (bf16[4,64,512]{2,1,0:T(8,128)(2,1)S(1)}, bf16[4,64,512]{2,1,0:T(8,128)(2,1)S(1)}, u32[]{:S(2)}, u32[]{:S(2)}) collective-permute-start(bf16[4,64,512]{2,1,0:T(8,128)(2,1)S(1)} %get-tuple-element.28.rest_0_), channel_id=1, source_target_pairs={{0,2},{2,0},{1,3},{3,1},{4,6},{6,4},{5,7},{7,5},{8,10},{10,8},{9,1... | collective-permute-start | bytes 786440 | tf_op jit(solution)/shard_map/ppermute | solution.py:308
  30.5 9.5 %collective-permute-start.3 = (bf16[4,64,512]{2,1,0:T(8,128)(2,1)S(1)}, bf16[4,64,512]{2,1,0:T(8,128)(2,1)S(1)}, u32[]{:S(2)}, u32[]{:S(2)}) collective-permute-start(bf16[4,64,512]{2,1,0:T(8,128)(2,1)S(1)} %get-tuple-element.28.rest_0_), channel_id=1, source_target_pairs={{0,16},{16,0},{1,17},{17,1},{2,18},{18,2},{3,19},{19,3},{4,20},{20... | collective-permute-start | bytes 786440 | tf_op jit(solution)/shard_map/ppermute | solution.py:308
  33.6 8.4 %collective-permute-start.8 = (bf16[4,64,512]{2,1,0:T(8,128)(2,1)S(1)}, bf16[4,64,512]{2,1,0:T(8,128)(2,1)S(1)}, u32[]{:S(2)}, u32[]{:S(2)}) collective-permute-start(bf16[4,64,512]{2,1,0:T(8,128)(2,1)S(1)} %collective-permute-done.5.rest_3_.rest_4_), channel_id=1, source_target_pairs={{0,8},{8,12},{12,4},{4,0},{1,9},{9,13},{13,5},{5,1},{2,10},{10,14}... | collective-permute-start | bytes 786440 | tf_op jit(solution)/shard_map/ppermute | solution.py:325
  36.9 10.7 %collective-permute-start.6 = (bf16[4,64,512]{2,1,0:T(8,128)(2,1)S(1)}, bf16[4,64,512]{2,1,0:T(8,128)(2,1)S(1)}, u32[]{:S(2)}, u32[]{:S(2)}) collective-permute-start(bf16[4,64,512]{2,1,0:T(8,128)(2,1)S(1)} %collective-permute-done.5.rest_3_.rest_4_), channel_id=1, source_target_pairs={{0,2},{2,0},{1,3},{3,1},{4,6},{6,4},{5,7},{7,5},{8,10},{10,8},{9,1... | collective-permute-start | bytes 786440 | tf_op jit(solution)/shard_map/ppermute | solution.py:308
  38.4 9.2 %collective-permute-start.4 = (bf16[4,64,512]{2,1,0:T(8,128)(2,1)S(1)}, bf16[4,64,512]{2,1,0:T(8,128)(2,1)S(1)}, u32[]{:S(2)}, u32[]{:S(2)}) collective-permute-start(bf16[4,64,512]{2,1,0:T(8,128)(2,1)S(1)} %collective-permute-done.2.rest_0_.rest_1_), channel_id=1, source_target_pairs={{0,16},{16,0},{1,17},{17,1},{2,18},{18,2},{3,19},{19,3},{4,20},{20... | collective-permute-start | bytes 786440 | tf_op jit(solution)/shard_map/ppermute | solution.py:308
  39.9 11.1 %collective-permute-start.7 = (bf16[4,64,512]{2,1,0:T(8,128)(2,1)S(1)}, bf16[4,64,512]{2,1,0:T(8,128)(2,1)S(1)}, u32[]{:S(2)}, u32[]{:S(2)}) collective-permute-start(bf16[4,64,512]{2,1,0:T(8,128)(2,1)S(1)} %collective-permute-done.5.rest_3_.rest_4_), channel_id=1, source_target_pairs={{0,16},{16,0},{1,17},{17,1},{2,18},{18,2},{3,19},{19,3},{4,20},{20... | collective-permute-start | bytes 786440 | tf_op jit(solution)/shard_map/ppermute | solution.py:308
  42.0 9.0 %collective-permute-start.9 = (bf16[4,64,512]{2,1,0:T(8,128)(2,1)S(1)}, bf16[4,64,512]{2,1,0:T(8,128)(2,1)S(1)}, u32[]{:S(2)}, u32[]{:S(2)}) collective-permute-start(bf16[4,64,512]{2,1,0:T(8,128)(2,1)S(1)} %collective-permute-done.8.rest_6_.rest_8_), channel_id=1, source_target_pairs={{0,8},{8,12},{12,4},{4,0},{1,9},{9,13},{13,5},{5,1},{2,10},{10,14}... | collective-permute-start | bytes 786440 | tf_op jit(solution)/shard_map/ppermute | solution.py:325
  47.7 13.5 %copy-start.3 = (bf16[4,64,512]{2,1,0:T(8,128)(2,1)}, bf16[4,64,512]{2,1,0:T(8,128)(2,1)S(1)}, u32[]{:S(2)}) copy-start(bf16[4,64,512]{2,1,0:T(8,128)(2,1)S(1)} %collective-permute-done.4.rest_2_.rest_3_) | copy-start | bytes 786436
  51.0 10.2 %copy-start.5 = (bf16[4,64,512]{2,1,0:T(8,128)(2,1)}, bf16[4,64,512]{2,1,0:T(8,128)(2,1)S(1)}, u32[]{:S(2)}) copy-start(bf16[4,64,512]{2,1,0:T(8,128)(2,1)S(1)} %collective-permute-done.7.rest_5_.rest_6_) | copy-start | bytes 786436
  51.0 13.5 %copy-start.7 = (bf16[4,64,512]{2,1,0:T(8,128)(2,1)}, bf16[4,64,512]{2,1,0:T(8,128)(2,1)S(1)}, u32[]{:S(2)}) copy-start(bf16[4,64,512]{2,1,0:T(8,128)(2,1)S(1)} %collective-permute-done.9.rest_7_.rest_12_) | copy-start | bytes 786436
  51.0 2.4 %copy-start.20 = (bf16[1,1024,2048]{2,1,0:T(8,128)(2,1)S(1)}, bf16[1,1024,2048]{2,1,0:T(8,128)(2,1)}, u32[]{:S(2)}) copy-start(bf16[1,1024,2048]{2,1,0:T(8,128)(2,1)} %get-tuple-element.26.w_in) | copy-start | bytes 12582916
  53.4 2.2 %copy-start.21 = (bf16[1,2048,1024]{2,1,0:T(8,128)(2,1)S(1)}, bf16[1,2048,1024]{2,1,0:T(8,128)(2,1)}, u32[]{:S(2)}) copy-start(bf16[1,2048,1024]{2,1,0:T(8,128)(2,1)} %get-tuple-element.27.w_out) | copy-start | bytes 12582916
  61.2 34.1 %copy-start.14 = (f32[1024]{0:T(1024)S(1)}, f32[1024]{0:T(1024)}, u32[]{:S(2)}) copy-start(f32[1024]{0:T(1024)} %param.22) | copy-start | bytes 12292
  61.2 34.1 %copy-start.16 = (s32[4,4]{1,0:T(4,128)S(1)}, s32[4,4]{1,0:T(4,128)}, u32[]{:S(2)}) copy-start(s32[4,4]{1,0:T(4,128)} %constant.2.clone.chips) | copy-start | bytes 196
  61.2 34.1 %copy-start.4 = (bf16[4,64,512]{2,1,0:T(8,128)(2,1)S(1)}, bf16[4,64,512]{2,1,0:T(8,128)(2,1)}, u32[]{:S(2)}) copy-start(bf16[4,64,512]{2,1,0:T(8,128)(2,1)} %copy-done.3) | copy-start | bytes 786436
  61.2 2.2 %collective-permute-start.12 = (bf16[320,1024]{1,0:T(8,128)(2,1)S(1)}, bf16[320,1024]{1,0:T(8,128)(2,1)S(1)}, u32[]{:S(2)}, u32[]{:S(2)}) collective-permute-start(bf16[320,1024]{1,0:T(8,128)(2,1)S(1)} %get-tuple-element.30), channel_id=1, source_target_pairs={{0,1},{1,0},{2,3},{3,2},{4,5},{5,4},{6,7},{7,6},{8,9},{9,8},{10,11... | collective-permute-start | bytes 1966088 | tf_op jit(solution)/shard_map/ppermute | solution.py:238
  64.5 22.0 %all-to-all-start.1 = ((bf16[8,40,1024]{2,1,0:T(8,128)(2,1)}), bf16[8,40,1024]{2,1,0:T(8,128)(2,1)S(1)}, u32[]{:S(2)}, u32[]{:S(2)}) async-start(bf16[8,40,1024]{2,1,0:T(8,128)(2,1)} %bitcast.15), calls=%async_computation.1 | async-start | bytes 1310720 | tf_op jit(solution)/shard_map/all_to_all | solution.py:428
  68.4 9.3 %collective-permute-start.16 = (bf16[4,64,512]{2,1,0:T(8,128)(2,1)S(1)}, bf16[4,64,512]{2,1,0:T(8,128)(2,1)}, u32[]{:S(2)}, u32[]{:S(2)}) collective-permute-start(bf16[4,64,512]{2,1,0:T(8,128)(2,1)S(1)} %collective-permute-done.8.rest_6_.rest_8_), channel_id=1, source_target_pairs={{0,16},{16,0},{1,17},{17,1},{2,18},{18,2},{3,19},{19,3},{4,20},{20... | collective-permute-start | bytes 786440 | tf_op jit(solution)/shard_map/ppermute | solution.py:308
  69.9 14.8 %collective-permute-start.18 = (bf16[4,64,512]{2,1,0:T(8,128)(2,1)}, bf16[4,64,512]{2,1,0:T(8,128)(2,1)}, u32[]{:S(2)}, u32[]{:S(2)}) collective-permute-start(bf16[4,64,512]{2,1,0:T(8,128)(2,1)} %copy-done.7), channel_id=1, source_target_pairs={{0,2},{2,0},{1,3},{3,1},{4,6},{6,4},{5,7},{7,5},{8,10},{10,8},{9,1... | collective-permute-start | bytes 786440 | tf_op jit(solution)/shard_map/ppermute | solution.py:308
  72.0 17.4 %collective-permute-start.14 = (bf16[4,64,512]{2,1,0:T(8,128)(2,1)S(1)}, bf16[4,64,512]{2,1,0:T(8,128)(2,1)}, u32[]{:S(2)}, u32[]{:S(2)}) collective-permute-start(bf16[4,64,512]{2,1,0:T(8,128)(2,1)S(1)} %collective-permute-done.6.rest_4_.rest_5_), channel_id=1, source_target_pairs={{0,16},{16,0},{1,17},{17,1},{2,18},{18,2},{3,19},{19,3},{4,20},{20... | collective-permute-start | bytes 786440 | tf_op jit(solution)/shard_map/ppermute | solution.py:308
  72.5 17.9 %collective-permute-start.15 = (bf16[4,64,512]{2,1,0:T(8,128)(2,1)S(1)}, bf16[4,64,512]{2,1,0:T(8,128)(2,1)}, u32[]{:S(2)}, u32[]{:S(2)}) collective-permute-start(bf16[4,64,512]{2,1,0:T(8,128)(2,1)S(1)} %collective-permute-done.8.rest_6_.rest_8_), channel_id=1, source_target_pairs={{0,2},{2,0},{1,3},{3,1},{4,6},{6,4},{5,7},{7,5},{8,10},{10,8},{9,1... | collective-permute-start | bytes 786440 | tf_op jit(solution)/shard_map/ppermute | solution.py:308
  72.5 22.8 %collective-permute-start.19 = (bf16[4,64,512]{2,1,0:T(8,128)(2,1)}, bf16[4,64,512]{2,1,0:T(8,128)(2,1)}, u32[]{:S(2)}, u32[]{:S(2)}) collective-permute-start(bf16[4,64,512]{2,1,0:T(8,128)(2,1)} %copy-done.7), channel_id=1, source_target_pairs={{0,16},{16,0},{1,17},{17,1},{2,18},{18,2},{3,19},{19,3},{4,20},{20... | collective-permute-start | bytes 786440 | tf_op jit(solution)/shard_map/ppermute | solution.py:308
  77.7 17.6 %collective-permute-start.17 = (bf16[4,64,512]{2,1,0:T(8,128)(2,1)}, bf16[4,64,512]{2,1,0:T(8,128)(2,1)}, u32[]{:S(2)}, u32[]{:S(2)}) collective-permute-start(bf16[4,64,512]{2,1,0:T(8,128)(2,1)} %collective-permute-done.16.rest_10_), channel_id=1, source_target_pairs={{0,2},{2,0},{1,3},{3,1},{4,6},{6,4},{5,7},{7,5},{8,10},{10,8},{9,1... | collective-permute-start | bytes 786440 | tf_op jit(solution)/shard_map/ppermute | solution.py:308
  84.8 10.5 %collective-permute-start.20 = (bf16[4,64,512]{2,1,0:T(8,128)(2,1)}, bf16[4,64,512]{2,1,0:T(8,128)(2,1)}, u32[]{:S(2)}, u32[]{:S(2)}) collective-permute-start(bf16[4,64,512]{2,1,0:T(8,128)(2,1)} %collective-permute-done.18.rest_13_), channel_id=1, source_target_pairs={{0,16},{16,0},{1,17},{17,1},{2,18},{18,2},{3,19},{19,3},{4,20},{20... | collective-permute-start | bytes 786440 | tf_op jit(solution)/shard_map/ppermute | solution.py:308
  86.5 0.9 copy-start.11
  87.4 0.9 copy-start.13
  89.4 10.2 %collective-permute-start.13 = (bf16[128,1024]{1,0:T(8,128)(2,1)}, bf16[128,1024]{1,0:T(8,128)(2,1)S(1)}, u32[]{:S(2)}, u32[]{:S(2)}) collective-permute-start(bf16[128,1024]{1,0:T(8,128)(2,1)} %get-tuple-element.21), channel_id=1, source_target_pairs={{0,1},{1,0},{2,3},{3,2},{4,5},{5,4},{6,7},{7,6},{8,9},{9,8},{10,11... | collective-permute-start | bytes 786440 | tf_op jit(solution)/shard_map/ppermute | solution.py:238
  95.3 1.0 copy-start.6
  96.3 0.9 copy-start.8
  97.2 6.8 %copy-start.19 = (s32[2]{0:T(128)S(1)}, s32[2]{0:T(128)}, u32[]{:S(2)}) copy-start(s32[2]{0:T(128)} %tgt_lengths.1) | copy-start | bytes 28
  102.4 1.6 %collective-permute-start.21 = (bf16[128,1024]{1,0:T(8,128)(2,1)S(1)}, bf16[128,1024]{1,0:T(8,128)(2,1)S(1)}, u32[]{:S(2)}, u32[]{:S(2)}) collective-permute-start(bf16[128,1024]{1,0:T(8,128)(2,1)S(1)} %get-tuple-element.43), channel_id=1, source_target_pairs={{0,1},{1,0},{2,3},{3,2},{4,5},{5,4},{6,7},{7,6},{8,9},{9,8},{10,11... | collective-permute-start | bytes 786440 | tf_op jit(solution)/shard_map/ppermute | solution.py:238

commit v3 on v2

--- a/solution.py
+++ b/solution.py
@@ -87,14 +87,31 @@
         copy.wait()
 
 
-def ffn_kernel(rows, others, w_in, w_out, *rest):
-    for source, out in ((others, rest[-1]), (rows, rest[-2])):
+def ffn_kernel(ahead, rows, others, w_in, w_out, *rest):
+    mine, theirs, held, sems = rest[ahead:]
+    units = w_in.shape[2]
+    block = min(units, FFN_BLOCK)
+    copies = [
+        pltpu.make_async_copy(w_out.at[0, pl.ds(n, block), :], held.at[pl.ds(n, block), :], sems.at[i])
+        for i, n in enumerate(range(0, units, block))
+    ]
+    for copy in copies:
+        copy.start()
+    both = [
+        [
+            jnp.maximum(
+                jnp.dot(source[...], w_in[0, :, n : n + block], preferred_element_type=F32), 0.0
+            ).astype(BF16)
+            for n in range(0, units, block)
+        ]
+        for source in (others, rows)
+    ]
+    for copy in copies:
+        copy.wait()
+    for hidden, out in zip(both, (theirs, mine)):
         total = None
-        block = min(w_in.shape[2], FFN_BLOCK)
-        for n in range(0, w_in.shape[2], block):
-            hidden = jnp.dot(source[...], w_in[0, :, n : n + block], preferred_element_type=F32)
-            hidden = jnp.maximum(hidden, 0.0).astype(BF16)
-            term = jnp.dot(hidden, w_out[0, n : n + block, :], preferred_element_type=F32)
+        for i, part in enumerate(hidden):
+            term = jnp.dot(part, held[i * block : (i + 1) * block, :], preferred_element_type=F32)
             total = term if total is None else total + term
         out[...] = total.astype(BF16)
 
@@ -170,6 +187,7 @@
 FAR = pl.BlockSpec(memory_space=pltpu.HBM)
 ANY = pl.BlockSpec(memory_space=pl.ANY)
 WIDE = pltpu.CompilerParams(vmem_limit_bytes=63 * 2**20)
+ROOM = pltpu.CompilerParams(vmem_limit_bytes=54 * 2**20)
 TIGHT = pltpu.CompilerParams(vmem_limit_bytes=51 * 2**20)
 NEAR = pltpu.CompilerParams(vmem_limit_bytes=24 * 2**20)
 
@@ -226,12 +244,28 @@
 
 def ffn(rows, others, w_in, w_out, ahead=()):
     shape = whole((rows.shape[0], w_out.shape[2]))
+    units = w_in.shape[2]
     return near(
-        ffn_kernel,
+        functools.partial(ffn_kernel, len(ahead)),
         (shape, shape), rows, others, w_in, w_out, *ahead,
-        specs={4 + i: ANY for i in range(len(ahead))},
-        flops=8 * rows.shape[0] * w_in.shape[1] * w_in.shape[2],
-    )
+        specs={3: FAR, **{4 + i: ANY for i in range(len(ahead))}},
+        scratch=[
+            pltpu.VMEM(w_out.shape[1:], BF16),
+            pltpu.SemaphoreType.DMA((units // min(units, FFN_BLOCK),)),
+        ],
+        flops=8 * rows.shape[0] * w_in.shape[1] * units,
+        params=ROOM,
+    )
+
+
+def after(block, others):
+    return pl.pallas_call(
+        lambda *refs: None,
+        in_specs=[ANY] * (1 + len(others)),
+        out_specs=ANY,
+        out_shape=whole(block.shape),
+        input_output_aliases={0: 0},
+    )(block, *others)
 
 
 def partner(block):
@@ -403,9 +437,12 @@
         ahead, choice = (), ()
         stacked = jnp.stack((w_query, w_key, w_value, w_attn))
         gathered = lax.all_gather(stacked, EXPERT, axis=0, tiled=False)
-    fetched = (w_in, w_out, sources, targets, targets)
+    arrived = lax.all_to_all(
+        outgoing.reshape(experts, capacity, width), CHIPS, split_axis=0, concat_axis=0, tiled=True
+    ).reshape(-1, width)
+    fetched = (w_in, sources, targets, targets)
     matrix = whole((tokens, experts * capacity))
-    w_in, w_out, *held, high, low = near(
+    w_in, *held, high, low = near(
         functools.partial(preload_kernel, experts, capacity, len(fetched), len(choice)),
         (*(whole(x.shape) for x in fetched), *(whole(x.shape) for x in choice[:1]), matrix, matrix),
         *fetched, *choice, ids, gates,
@@ -415,12 +452,9 @@
     )
     if by_pairs:
         *held, piece = held
-        pieces = gather_pieces(piece)
+        pieces = gather_pieces(after(piece, [arrived]))
         others, other_lengths = partner(targets), partner(src_lengths)
         ahead = [pieces[i] for i in AHEAD] + [others, other_lengths]
-    arrived = lax.all_to_all(
-        outgoing.reshape(experts, capacity, width), CHIPS, split_axis=0, concat_axis=0, tiled=True
-    ).reshape(-1, width)
     mine, theirs = ffn(arrived, partner(arrived), w_in, w_out, ahead)
     if heads > 1:
         mine, theirs = (lax.psum(x.astype(F32), "head").astype(BF16) for x in (mine, theirs))

time: 106 us -> 109 us (1.028)
  waiting for transfers between devices: 29.5 us -> 35.5 us
  starting transfers between devices: 37.4 us -> 33.8 us
  local copies, waits for them, and re-layouts: 13.8 us -> 11.8 us
  other arithmetic: 1.1 us -> 2.21 us
  Pallas kernels: 22.9 us -> 24 us
    all_to_all x1, waiting for transfers between devices: 0.29 us -> 5.14 us  [shards(): lax.all_to_all(outgoing.reshape(experts, capacity, width), CHIPS, split_a...]
    ppermute x3, starting transfers between devices: 9.66 us -> 5.65 us  [gather_pieces(): piece = lax.ppermute(piece, 'hi', ring)]
    unnamed x44 -> x76, local copies, waits for them, and re-layouts: 13.8 us -> 11.8 us
    convert_element_type x1, other arithmetic: 1.1 us -> 2.21 us  [shards(): half = (mine.astype(F32) + partner(theirs).astype(F32)).astype(BF16)]
  transfers between devices with their start and end apart: 24 -> 24, of which waited for: 13 -> 13; matrix products, arithmetic and copies ran while one was open for 0% -> 0% of each run, Pallas kernels for 10% -> 7%
where the time goes in v3:
time: 109 us; the launch traced here: 108 us
  waiting for transfers between devices  35.5 us (33%)
  starting transfers between devices  33.8 us (31%)
  Pallas kernels  24 us (22%)
  local copies, waits for them, and re-layouts  11.8 us (11%)
  other arithmetic  2.21 us (2%)
    pallas_call x6, Pallas kernels, near(): pl.pallas_call(kernel, in_specs=[specs.get(i, SMEM if i < tables else HER...  21.2 us
    ppermute x12, waiting for transfers between devices, swap(): return lax.ppermute(block, axis, [(0, 1), (1, 0)])  20.6 us
    ppermute x12, starting transfers between devices, swap(): return lax.ppermute(block, axis, [(0, 1), (1, 0)])  15.8 us
    unnamed x76, local copies, waits for them, and re-layouts  11.8 us
    all_to_all x1, starting transfers between devices, shards(): lax.all_to_all(outgoing.reshape(experts, capacity, width), CHIPS, split_a...  7.39 us
    ppermute x7, waiting for transfers between devices, partner(): return lax.ppermute(block, 'pair', [(0, 1), (1, 0)])  5.98 us
    ppermute x3, starting transfers between devices, gather_pieces(): piece = lax.ppermute(piece, 'hi', ring)  5.65 us
    all_to_all x1, waiting for transfers between devices, shards(): lax.all_to_all(outgoing.reshape(experts, capacity, width), CHIPS, split_a...  5.14 us
  transfers between devices with their start and end apart: 24, of which 13 were waited for; matrix products, arithmetic and copies ran while one was open for 0% of the time, Pallas kernels for 7%

profile of v3, /device:TPU:0, one launch (start us, length us, event | category | flops | bytes accessed | tf_op | source)
XLA Modules:
  0.0 108.3 jit_solution(2043631283669541390)
XLA Ops:
  0.6 2.8 %shard_map.158 = (bf16[320,1024]{1,0:T(8,128)(2,1)}, bf16[4,64,512]{2,1,0:T(8,128)(2,1)}, bf16[4,64,512]{2,1,0:T(8,128)(2,1)}) custom-call(bf16[128,1024]{1,0:T(8,128)(2,1)} %refs_1_.1, f32[1,1024]{1,0:T(1,128)} %bitcast.18, s32[2,128]{1,0:T(2,128)} %bitcast.10, bf16[64,1024]{1,0:T(8,128)(2,1)} %refs_3_.2, bf16[64,1024]{1,0:T(8,128)(2,1)} %refs_4_.1, ...), custom_call_target="tpu_custom_call" | custom-call | bytes 791552 | tf_op jit(solution)/shard_map/pallas_call | solution.py:219
  3.5 0.0 copy-start.1
  3.5 0.0 copy-start.32
  3.5 7.4 %all-to-all-start = ((bf16[8,40,1024]{2,1,0:T(8,128)(2,1)}), bf16[8,40,1024]{2,1,0:T(8,128)(2,1)S(1)}, u32[]{:S(2)}, u32[]{:S(2)}) async-start(bf16[8,40,1024]{2,1,0:T(8,128)(2,1)} %bitcast.17), calls=%async_computation | async-start | bytes 1310720 | tf_op jit(solution)/shard_map/all_to_all | solution.py:440
  10.9 1.7 %collective-permute-done.1.refs_5_ = bf16[4,64,512]{2,1,0:T(8,128)(2,1)S(1)} collective-permute-done((bf16[4,64,512]{2,1,0:T(8,128)(2,1)}, bf16[4,64,512]{2,1,0:T(8,128)(2,1)S(1)}, u32[]{:S(2)}, u32[]{:S(2)}) %collective-permute-start.1) | collective-permute-done | bytes 262176 | tf_op jit(solution)/shard_map/ppermute | solution.py:272
  12.6 0.9 copy-done
  13.6 0.9 copy-done.2
  14.5 0.9 copy-done.23
  15.5 0.7 copy-done.29
  16.1 0.7 copy-done.31
  16.8 4.2 %shard_map.159 = (bf16[1,1024,2048]{2,1,0:T(8,128)(2,1)}, bf16[128,1024]{1,0:T(8,128)(2,1)S(1)}, bf16[128,1024]{1,0:T(8,128)(2,1)S(1)}, bf16[128,1024]{1,0:T(8,1...) custom-call(bf16[1,1024,2048]{2,1,0:T(8,128)(2,1)} %refs_0_.3, ...), custom_call_target="tpu_custom_call" | custom-call | bytes 5507072 | tf_op jit(solution)/shard_map/pallas_call | solution.py:234
  21.0 0.0 copy-start.3
  21.1 0.7 copy-done.3
  21.7 0.6 copy-done.24
  22.4 0.6 copy-done.26
  23.0 5.1 %all-to-all-done = bf16[8,40,1024]{2,1,0:T(8,128)(2,1)S(1)} async-done(((bf16[8,40,1024]{2,1,0:T(8,128)(2,1)}), bf16[8,40,1024]{2,1,0:T(8,128)(2,1)S(1)}, u32[]{:S(2)}, u32[]{:S(2)}) %all-to-all-start) | async-done | bytes 655392 | tf_op jit(solution)/shard_map/all_to_all | solution.py:440
  28.2 0.9 copy-done.36
  29.0 0.0 collective-permute-start.5
  29.1 0.5 collective-permute-start.10
  29.6 0.1 collective-permute-start.11
  29.6 1.5 %collective-permute-start.2 = (bf16[4,64,512]{2,1,0:T(8,128)(2,1)}, bf16[4,64,512]{2,1,0:T(8,128)(2,1)S(1)}, u32[]{:S(2)}, u32[]{:S(2)}) collective-permute-start(bf16[4,64,512]{2,1,0:T(8,128)(2,1)} %shard_map.160.rest_0_), channel_id=1, source_target_pairs={{0,2},{2,0},{1,3},{3,1},{4,6},{6,4},{5,7},{7,5},{8,10},{10,8},{9,1... | collective-permute-start | bytes 786440 | tf_op jit(solution)/shard_map/ppermute | solution.py:342
  31.1 0.4 collective-permute-done.11.rest_9_.other_lengths
  31.5 1.5 %collective-permute-start.3 = (bf16[4,64,512]{2,1,0:T(8,128)(2,1)}, bf16[4,64,512]{2,1,0:T(8,128)(2,1)S(1)}, u32[]{:S(2)}, u32[]{:S(2)}) collective-permute-start(bf16[4,64,512]{2,1,0:T(8,128)(2,1)} %shard_map.160.rest_0_), channel_id=1, source_target_pairs={{0,16},{16,0},{1,17},{17,1},{2,18},{18,2},{3,19},{19,3},{4,20},{20... | collective-permute-start | bytes 786440 | tf_op jit(solution)/shard_map/ppermute | solution.py:342
  33.0 2.8 %collective-permute-done.5.rest_3_.rest_4_ = bf16[4,64,512]{2,1,0:T(8,128)(2,1)S(1)} collective-permute-done((bf16[4,64,512]{2,1,0:T(8,128)(2,1)}, bf16[4,64,512]{2,1,0:T(8,128)(2,1)S(1)}, u32[]{:S(2)}, u32[]{:S(2)}) %collective-permute-start.5) | collective-permute-done | bytes 262176 | tf_op jit(solution)/shard_map/ppermute | solution.py:359
  35.8 2.3 %collective-permute-start.8 = (bf16[4,64,512]{2,1,0:T(8,128)(2,1)S(1)}, bf16[4,64,512]{2,1,0:T(8,128)(2,1)S(1)}, u32[]{:S(2)}, u32[]{:S(2)}) collective-permute-start(bf16[4,64,512]{2,1,0:T(8,128)(2,1)S(1)} %collective-permute-done.5.rest_3_.rest_4_), channel_id=1, source_target_pairs={{0,8},{8,12},{12,4},{4,0},{1,9},{9,13},{13,5},{5,1},{2,10},{10,14}... | collective-permute-start | bytes 786440 | tf_op jit(solution)/shard_map/ppermute | solution.py:359
  38.1 1.1 collective-permute-start.6
  39.2 1.5 %collective-permute-start.4 = (bf16[4,64,512]{2,1,0:T(8,128)(2,1)S(1)}, bf16[4,64,512]{2,1,0:T(8,128)(2,1)S(1)}, u32[]{:S(2)}, u32[]{:S(2)}) collective-permute-start(bf16[4,64,512]{2,1,0:T(8,128)(2,1)S(1)} %collective-permute-done.2.rest_0_.rest_1_), channel_id=1, source_target_pairs={{0,16},{16,0},{1,17},{17,1},{2,18},{18,2},{3,19},{19,3},{4,20},{20... | collective-permute-start | bytes 786440 | tf_op jit(solution)/shard_map/ppermute | solution.py:342
  40.7 0.9 collective-permute-start.7
  41.6 1.0 collective-permute-done.8.rest_6_.rest_8_
  42.6 3.4 %collective-permute-start.9 = (bf16[4,64,512]{2,1,0:T(8,128)(2,1)S(1)}, bf16[4,64,512]{2,1,0:T(8,128)(2,1)S(1)}, u32[]{:S(2)}, u32[]{:S(2)}) collective-permute-start(bf16[4,64,512]{2,1,0:T(8,128)(2,1)S(1)} %collective-permute-done.8.rest_6_.rest_8_), channel_id=1, source_target_pairs={{0,8},{8,12},{12,4},{4,0},{1,9},{9,13},{13,5},{5,1},{2,10},{10,14}... | collective-permute-start | bytes 786440 | tf_op jit(solution)/shard_map/ppermute | solution.py:359
  46.0 2.4 %collective-permute-done.4.rest_2_.rest_3_ = bf16[4,64,512]{2,1,0:T(8,128)(2,1)S(1)} collective-permute-done((bf16[4,64,512]{2,1,0:T(8,128)(2,1)S(1)}, bf16[4,64,512]{2,1,0:T(8,128)(2,1)S(1)}, u32[]{:S(2)}, u32[]{:S(2)}) %collective-permute-start.4) | collective-permute-done | bytes 262176 | tf_op jit(solution)/shard_map/ppermute | solution.py:342
  48.4 3.5 %collective-permute-done.7.rest_5_.rest_6_ = bf16[4,64,512]{2,1,0:T(8,128)(2,1)S(1)} collective-permute-done((bf16[4,64,512]{2,1,0:T(8,128)(2,1)S(1)}, bf16[4,64,512]{2,1,0:T(8,128)(2,1)S(1)}, u32[]{:S(2)}, u32[]{:S(2)}) %collective-permute-start.7) | collective-permute-done | bytes 262176 | tf_op jit(solution)/shard_map/ppermute | solution.py:342
  52.1 0.6 copy-done.19
  52.7 0.2 copy-done.37
  52.9 0.1 copy-done.21
  53.0 9.2 %shard_map.161 = (bf16[320,1024]{1,0:T(8,128)(2,1)}, bf16[320,1024]{1,0:T(8,128)(2,1)}) custom-call(bf16[320,1024]{1,0:T(8,128)(2,1)} %bitcast.15, bf16[320,1024]{1,0:T(8,128)(2,1)} %copy-done.37, bf16[1,1024,2048]{2,1,0:T(8,128)(2,1)} %get-tuple-element.25.w_in, bf16[1,2048,1024]{2,1,0:T(8,128)(2,1)} %w_out.1, bf16[4,64,512]{2,1,0:T(8,128)(2,1)} %copy-done.9, ...), custom_call_target="tpu_custom_call" | custom-call | flops 5368709120 | bytes 12058632 | tf_op jit(solution)/shard_map/pallas_call | solution.py:234
  62.3 0.0 copy-start.4
  62.3 0.0 copy-start.28
  62.3 0.0 copy-start.30
  62.4 0.1 collective-permute-start.12
  62.4 2.3 %collective-permute-done.12 = bf16[320,1024]{1,0:T(8,128)(2,1)S(1)} collective-permute-done((bf16[320,1024]{1,0:T(8,128)(2,1)}, bf16[320,1024]{1,0:T(8,128)(2,1)S(1)}, u32[]{:S(2)}, u32[]{:S(2)}) %collective-permute-start.12) | collective-permute-done | bytes 655392 | tf_op jit(solution)/shard_map/ppermute | solution.py:272
  64.7 2.2 %add_convert_fusion = bf16[320,1024]{1,0:T(8,128)(2,1)} fusion(bf16[320,1024]{1,0:T(8,128)(2,1)S(1)} %collective-permute-done.12, bf16[320,1024]{1,0:T(8,128)(2,1)} %get-tuple-element.27), kind=kLoop, calls=%fused_computation | loop fusion | flops 1310720 | bytes 1966080 | tf_op jit(solution)/shard_map/convert_element_type | solution.py:461
  67.0 4.2 %all-to-all-start.1 = ((bf16[8,40,1024]{2,1,0:T(8,128)(2,1)}), bf16[8,40,1024]{2,1,0:T(8,128)(2,1)S(1)}, u32[]{:S(2)}, u32[]{:S(2)}) async-start(bf16[8,40,1024]{2,1,0:T(8,128)(2,1)} %bitcast.16), calls=%async_computation.1 | async-start | bytes 1310720 | tf_op jit(solution)/shard_map/all_to_all | solution.py:462
  71.2 1.5 %collective-permute-start.16 = (bf16[4,64,512]{2,1,0:T(8,128)(2,1)}, bf16[4,64,512]{2,1,0:T(8,128)(2,1)}, u32[]{:S(2)}, u32[]{:S(2)}) collective-permute-start(bf16[4,64,512]{2,1,0:T(8,128)(2,1)} %copy-done.13), channel_id=1, source_target_pairs={{0,16},{16,0},{1,17},{17,1},{2,18},{18,2},{3,19},{19,3},{4,20},{20... | collective-permute-start | bytes 786440 | tf_op jit(solution)/shard_map/ppermute | solution.py:342
  72.7 2.0 %collective-permute-start.18 = (bf16[4,64,512]{2,1,0:T(8,128)(2,1)}, bf16[4,64,512]{2,1,0:T(8,128)(2,1)}, u32[]{:S(2)}, u32[]{:S(2)}) collective-permute-start(bf16[4,64,512]{2,1,0:T(8,128)(2,1)} %copy-done.21), channel_id=1, source_target_pairs={{0,2},{2,0},{1,3},{3,1},{4,6},{6,4},{5,7},{7,5},{8,10},{10,8},{9,1... | collective-permute-start | bytes 786440 | tf_op jit(solution)/shard_map/ppermute | solution.py:342
  74.7 0.5 collective-permute-start.14
  75.2 0.0 collective-permute-start.15
  75.2 1.5 %collective-permute-start.19 = (bf16[4,64,512]{2,1,0:T(8,128)(2,1)}, bf16[4,64,512]{2,1,0:T(8,128)(2,1)}, u32[]{:S(2)}, u32[]{:S(2)}) collective-permute-start(bf16[4,64,512]{2,1,0:T(8,128)(2,1)} %copy-done.21), channel_id=1, source_target_pairs={{0,16},{16,0},{1,17},{17,1},{2,18},{18,2},{3,19},{19,3},{4,20},{20... | collective-permute-start | bytes 786440 | tf_op jit(solution)/shard_map/ppermute | solution.py:342
  76.7 3.9 %collective-permute-done.16.rest_10_ = bf16[4,64,512]{2,1,0:T(8,128)(2,1)} collective-permute-done((bf16[4,64,512]{2,1,0:T(8,128)(2,1)}, bf16[4,64,512]{2,1,0:T(8,128)(2,1)}, u32[]{:S(2)}, u32[]{:S(2)}) %collective-permute-start.16) | collective-permute-done | bytes 262176 | tf_op jit(solution)/shard_map/ppermute | solution.py:342
  80.7 2.1 %collective-permute-start.17 = (bf16[4,64,512]{2,1,0:T(8,128)(2,1)}, bf16[4,64,512]{2,1,0:T(8,128)(2,1)}, u32[]{:S(2)}, u32[]{:S(2)}) collective-permute-start(bf16[4,64,512]{2,1,0:T(8,128)(2,1)} %collective-permute-done.16.rest_10_), channel_id=1, source_target_pairs={{0,2},{2,0},{1,3},{3,1},{4,6},{6,4},{5,7},{7,5},{8,10},{10,8},{9,1... | collective-permute-start | bytes 786440 | tf_op jit(solution)/shard_map/ppermute | solution.py:342
  82.7 4.8 %collective-permute-done.18.rest_13_ = bf16[4,64,512]{2,1,0:T(8,128)(2,1)} collective-permute-done((bf16[4,64,512]{2,1,0:T(8,128)(2,1)}, bf16[4,64,512]{2,1,0:T(8,128)(2,1)}, u32[]{:S(2)}, u32[]{:S(2)}) %collective-permute-start.18) | collective-permute-done | bytes 262176 | tf_op jit(solution)/shard_map/ppermute | solution.py:342
  87.5 1.7 %collective-permute-start.20 = (bf16[4,64,512]{2,1,0:T(8,128)(2,1)}, bf16[4,64,512]{2,1,0:T(8,128)(2,1)}, u32[]{:S(2)}, u32[]{:S(2)}) collective-permute-start(bf16[4,64,512]{2,1,0:T(8,128)(2,1)} %collective-permute-done.18.rest_13_), channel_id=1, source_target_pairs={{0,16},{16,0},{1,17},{17,1},{2,18},{18,2},{3,19},{19,3},{4,20},{20... | collective-permute-start | bytes 786440 | tf_op jit(solution)/shard_map/ppermute | solution.py:342
  89.2 0.9 copy-done.25
  90.1 0.9 copy-done.27
  91.0 1.1 %shard_map.162 = (bf16[128,1024]{1,0:T(8,128)(2,1)}, bf16[128,1024]{1,0:T(8,128)(2,1)S(1)}) custom-call(bf16[320,1024]{1,0:T(8,128)(2,1)S(1)} %bitcast.8, bf16[128,320]{1,0:T(8,128)(2,1)S(1)} %copy-done.25, bf16[128,320]{1,0:T(8,128)(2,1)S(1)} %copy-done.27, bf16[128,1024]{1,0:T(8,128)(2,1)S(1)} %get-tuple-element.31.sources), custom_call_target="tpu_custom_call" | custom-call | bytes 1081344 | tf_op jit(solution)/shard_map/pallas_call | solution.py:234
  92.2 1.0 collective-permute-done.15.rest_9_
  93.2 4.9 %collective-permute-done.17.rest_11_ = bf16[4,64,512]{2,1,0:T(8,128)(2,1)} collective-permute-done((bf16[4,64,512]{2,1,0:T(8,128)(2,1)}, bf16[4,64,512]{2,1,0:T(8,128)(2,1)}, u32[]{:S(2)}, u32[]{:S(2)}) %collective-permute-start.17) | collective-permute-done | bytes 262176 | tf_op jit(solution)/shard_map/ppermute | solution.py:342
  98.2 0.9 copy-done.20
  99.1 0.9 copy-done.22
  100.0 2.3 %shard_map.163 = (bf16[256,512]{1,0:T(8,128)(2,1)S(1)}, bf16[1024,512]{1,0:T(8,128)(2,1)S(1)}, bf16[1024,512]{1,0:T(8,128)(2,1)S(1)}, bf16[1024,512]{1,0:T(8,128)(2,1)S(1)}) custom-call(s32[4,4]{1,0:T(4,128)S(1)} %copy-done.30, bf16[128,1024]{1,0:T(8,128)(2,1)S(1)} %get-tuple-element.35.targets, bf16[128,1024]{1,0:T(8,128)(2,1)S(1)} %copy-done.8, ...), custom_call_target="tpu_custom_call" | custom-call | bytes 4722752 | tf_op jit(solution)/shard_map/pallas_call | solution.py:234
  102.4 2.9 %shard_map.164 = (f32[128,1024]{1,0:T(8,128)S(1)}, bf16[128,1024]{1,0:T(8,128)(2,1)S(1)}) custom-call(s32[2]{0:T(128)S(1)} %copy-done.32, s32[2]{0:T(128)S(1)} %copy-done.35, bf16[128,1024]{1,0:T(8,128)(2,1)S(1)} %get-tuple-element.34.memory, bf16[128,1024]{1,0:T(8,128)(2,1)S(1)} %collective-permute-done.13.others, ...), custom_call_target="tpu_custom_call" | custom-call | bytes 3932176 | tf_op jit(solution)/shard_map/pallas_call | solution.py:234
  105.3 0.1 collective-permute-start.21
  105.4 1.5 %collective-permute-done.21.received = bf16[128,1024]{1,0:T(8,128)(2,1)S(1)} collective-permute-done((bf16[128,1024]{1,0:T(8,128)(2,1)S(1)}, bf16[128,1024]{1,0:T(8,128)(2,1)S(1)}, u32[]{:S(2)}, u32[]{:S(2)}) %collective-permute-start.21) | collective-permute-done | bytes 262176 | tf_op jit(solution)/shard_map/ppermute | solution.py:272
  106.9 1.4 %shard_map.165 = bf16[128,1024]{1,0:T(8,128)(2,1)} custom-call(s32[2]{0:T(128)S(1)} %copy-done.33, bf16[128,1024]{1,0:T(8,128)(2,1)S(1)} %get-tuple-element.33.targets, f32[128,1024]{1,0:T(8,128)S(1)} %get-tuple-element.40.kept, bf16[128,1024]{1,0:T(8,128)(2,1)S(1)} %collective-permute-done.21.received), custom_call_target="tpu_custom_call" | custom-call | bytes 1048584 | tf_op jit(solution)/shard_map/pallas_call | solution.py:234
  (69 shorter events, 0.1 us)
Async XLA Ops:
  3.5 25.6 %copy-start.1 = (bf16[128,1024]{1,0:T(8,128)(2,1)S(1)}, bf16[128,1024]{1,0:T(8,128)(2,1)}, u32[]{:S(2)}) copy-start(bf16[128,1024]{1,0:T(8,128)(2,1)} %refs_3_.3) | copy-start | bytes 786436
  3.5 26.1 %copy-start.32 = (s32[2]{0:T(128)S(1)}, s32[2]{0:T(128)}, u32[]{:S(2)}) copy-start(s32[2]{0:T(128)} %lengths.1) | copy-start | bytes 28
  3.5 24.7 %all-to-all-start = ((bf16[8,40,1024]{2,1,0:T(8,128)(2,1)}), bf16[8,40,1024]{2,1,0:T(8,128)(2,1)S(1)}, u32[]{:S(2)}, u32[]{:S(2)}) async-start(bf16[8,40,1024]{2,1,0:T(8,128)(2,1)} %bitcast.17), calls=%async_computation | async-start | bytes 1310720 | tf_op jit(solution)/shard_map/all_to_all | solution.py:440
  10.9 1.7 %collective-permute-start.1 = (bf16[4,64,512]{2,1,0:T(8,128)(2,1)}, bf16[4,64,512]{2,1,0:T(8,128)(2,1)S(1)}, u32[]{:S(2)}, u32[]{:S(2)}) collective-permute-start(bf16[4,64,512]{2,1,0:T(8,128)(2,1)} %get-tuple-element.24), channel_id=1, source_target_pairs={{0,1},{1,0},{2,3},{3,2},{4,5},{5,4},{6,7},{7,6},{8,9},{9,8},{10,11... | collective-permute-start | bytes 786440 | tf_op jit(solution)/shard_map/ppermute | solution.py:272
  12.6 1.0 copy-start
  13.6 0.9 copy-start.2
  14.5 0.9 copy-start.23
  15.5 0.7 copy-start.29
  16.1 0.7 copy-start.31
  21.0 0.7 copy-start.3
  21.7 0.6 copy-start.24
  22.4 0.6 copy-start.26
  28.2 0.9 copy-start.36
  29.0 6.8 %collective-permute-start.5 = (bf16[4,64,512]{2,1,0:T(8,128)(2,1)}, bf16[4,64,512]{2,1,0:T(8,128)(2,1)S(1)}, u32[]{:S(2)}, u32[]{:S(2)}) collective-permute-start(bf16[4,64,512]{2,1,0:T(8,128)(2,1)} %shard_map.160.rest_0_), channel_id=1, source_target_pairs={{0,8},{8,12},{12,4},{4,0},{1,9},{9,13},{13,5},{5,1},{2,10},{10,14}... | collective-permute-start | bytes 786440 | tf_op jit(solution)/shard_map/ppermute | solution.py:359
  29.0 22.9 %collective-permute-start = (bf16[320,1024]{1,0:T(8,128)(2,1)}, bf16[320,1024]{1,0:T(8,128)(2,1)S(1)}, u32[]{:S(2)}, u32[]{:S(2)}) collective-permute-start(bf16[320,1024]{1,0:T(8,128)(2,1)} %bitcast.14), channel_id=1, source_target_pairs={{0,1},{1,0},{2,3},{3,2},{4,5},{5,4},{6,7},{7,6},{8,9},{9,8},{10,11... | collective-permute-start | bytes 1966088 | tf_op jit(solution)/shard_map/ppermute | solution.py:272
  29.1 9.0 %collective-permute-start.10 = (bf16[128,1024]{1,0:T(8,128)(2,1)S(1)}, bf16[128,1024]{1,0:T(8,128)(2,1)S(1)}, u32[]{:S(2)}, u32[]{:S(2)}) collective-permute-start(bf16[128,1024]{1,0:T(8,128)(2,1)S(1)} %copy-done.1), channel_id=1, source_target_pairs={{0,1},{1,0},{2,3},{3,2},{4,5},{5,4},{6,7},{7,6},{8,9},{9,8},{10,11... | collective-permute-start | bytes 786440 | tf_op jit(solution)/shard_map/ppermute | solution.py:272
  29.6 2.0 %collective-permute-start.11 = (s32[2]{0:T(128)S(1)}, s32[2]{0:T(128)S(1)}, u32[]{:S(2)}, u32[]{:S(2)}) collective-permute-start(s32[2]{0:T(128)S(1)} %copy-done.32), channel_id=1, source_target_pairs={{0,1},{1,0},{2,3},{3,2},{4,5},{5,4},{6,7},{7,6},{8,9},{9,8},{10,11... | collective-permute-start | bytes 32 | tf_op jit(solution)/shard_map/ppermute | solution.py:272
  29.6 9.5 %collective-permute-start.2 = (bf16[4,64,512]{2,1,0:T(8,128)(2,1)}, bf16[4,64,512]{2,1,0:T(8,128)(2,1)S(1)}, u32[]{:S(2)}, u32[]{:S(2)}) collective-permute-start(bf16[4,64,512]{2,1,0:T(8,128)(2,1)} %shard_map.160.rest_0_), channel_id=1, source_target_pairs={{0,2},{2,0},{1,3},{3,1},{4,6},{6,4},{5,7},{7,5},{8,10},{10,8},{9,1... | collective-permute-start | bytes 786440 | tf_op jit(solution)/shard_map/ppermute | solution.py:342
  31.5 20.5 %copy-start.34 = (s32[2]{0:T(128)}, s32[2]{0:T(128)S(1)}, u32[]{:S(2)}) copy-start(s32[2]{0:T(128)S(1)} %collective-permute-done.11.rest_9_.other_lengths) | copy-start | bytes 28
  31.5 9.2 %collective-permute-start.3 = (bf16[4,64,512]{2,1,0:T(8,128)(2,1)}, bf16[4,64,512]{2,1,0:T(8,128)(2,1)S(1)}, u32[]{:S(2)}, u32[]{:S(2)}) collective-permute-start(bf16[4,64,512]{2,1,0:T(8,128)(2,1)} %shard_map.160.rest_0_), channel_id=1, source_target_pairs={{0,16},{16,0},{1,17},{17,1},{2,18},{18,2},{3,19},{19,3},{4,20},{20... | collective-permute-start | bytes 786440 | tf_op jit(solution)/shard_map/ppermute | solution.py:342
  35.8 16.2 %copy-start.5 = (bf16[4,64,512]{2,1,0:T(8,128)(2,1)}, bf16[4,64,512]{2,1,0:T(8,128)(2,1)S(1)}, u32[]{:S(2)}) copy-start(bf16[4,64,512]{2,1,0:T(8,128)(2,1)S(1)} %collective-permute-done.5.rest_3_.rest_4_) | copy-start | bytes 786436
  35.8 6.8 %collective-permute-start.8 = (bf16[4,64,512]{2,1,0:T(8,128)(2,1)S(1)}, bf16[4,64,512]{2,1,0:T(8,128)(2,1)S(1)}, u32[]{:S(2)}, u32[]{:S(2)}) collective-permute-start(bf16[4,64,512]{2,1,0:T(8,128)(2,1)S(1)} %collective-permute-done.5.rest_3_.rest_4_), channel_id=1, source_target_pairs={{0,8},{8,12},{12,4},{4,0},{1,9},{9,13},{13,5},{5,1},{2,10},{10,14}... | collective-permute-start | bytes 786440 | tf_op jit(solution)/shard_map/ppermute | solution.py:359
  38.1 13.9 %copy-start.7 = (bf16[128,1024]{1,0:T(8,128)(2,1)}, bf16[128,1024]{1,0:T(8,128)(2,1)S(1)}, u32[]{:S(2)}) copy-start(bf16[128,1024]{1,0:T(8,128)(2,1)S(1)} %collective-permute-done.10.rest_8_.others) | copy-start | bytes 786436
  38.1 10.3 %collective-permute-start.6 = (bf16[4,64,512]{2,1,0:T(8,128)(2,1)S(1)}, bf16[4,64,512]{2,1,0:T(8,128)(2,1)S(1)}, u32[]{:S(2)}, u32[]{:S(2)}) collective-permute-start(bf16[4,64,512]{2,1,0:T(8,128)(2,1)S(1)} %collective-permute-done.5.rest_3_.rest_4_), channel_id=1, source_target_pairs={{0,2},{2,0},{1,3},{3,1},{4,6},{6,4},{5,7},{7,5},{8,10},{10,8},{9,1... | collective-permute-start | bytes 786440 | tf_op jit(solution)/shard_map/ppermute | solution.py:342
  39.2 12.9 %copy-start.9 = (bf16[4,64,512]{2,1,0:T(8,128)(2,1)}, bf16[4,64,512]{2,1,0:T(8,128)(2,1)S(1)}, u32[]{:S(2)}) copy-start(bf16[4,64,512]{2,1,0:T(8,128)(2,1)S(1)} %collective-permute-done.2.rest_0_.rest_1_) | copy-start | bytes 786436
  39.2 9.2 %collective-permute-start.4 = (bf16[4,64,512]{2,1,0:T(8,128)(2,1)S(1)}, bf16[4,64,512]{2,1,0:T(8,128)(2,1)S(1)}, u32[]{:S(2)}, u32[]{:S(2)}) collective-permute-start(bf16[4,64,512]{2,1,0:T(8,128)(2,1)S(1)} %collective-permute-done.2.rest_0_.rest_1_), channel_id=1, source_target_pairs={{0,16},{16,0},{1,17},{17,1},{2,18},{18,2},{3,19},{19,3},{4,20},{20... | collective-permute-start | bytes 786440 | tf_op jit(solution)/shard_map/ppermute | solution.py:342
  40.7 11.3 %copy-start.11 = (bf16[4,64,512]{2,1,0:T(8,128)(2,1)}, bf16[4,64,512]{2,1,0:T(8,128)(2,1)S(1)}, u32[]{:S(2)}) copy-start(bf16[4,64,512]{2,1,0:T(8,128)(2,1)S(1)} %collective-permute-done.3.rest_1_.rest_2_) | copy-start | bytes 786436
  40.7 11.3 %collective-permute-start.7 = (bf16[4,64,512]{2,1,0:T(8,128)(2,1)S(1)}, bf16[4,64,512]{2,1,0:T(8,128)(2,1)S(1)}, u32[]{:S(2)}, u32[]{:S(2)}) collective-permute-start(bf16[4,64,512]{2,1,0:T(8,128)(2,1)S(1)} %collective-permute-done.5.rest_3_.rest_4_), channel_id=1, source_target_pairs={{0,16},{16,0},{1,17},{17,1},{2,18},{18,2},{3,19},{19,3},{4,20},{20... | collective-permute-start | bytes 786440 | tf_op jit(solution)/shard_map/ppermute | solution.py:342
  42.6 9.4 %copy-start.13 = (bf16[4,64,512]{2,1,0:T(8,128)(2,1)}, bf16[4,64,512]{2,1,0:T(8,128)(2,1)S(1)}, u32[]{:S(2)}) copy-start(bf16[4,64,512]{2,1,0:T(8,128)(2,1)S(1)} %collective-permute-done.8.rest_6_.rest_8_) | copy-start | bytes 786436
  42.6 9.3 %collective-permute-start.9 = (bf16[4,64,512]{2,1,0:T(8,128)(2,1)S(1)}, bf16[4,64,512]{2,1,0:T(8,128)(2,1)S(1)}, u32[]{:S(2)}, u32[]{:S(2)}) collective-permute-start(bf16[4,64,512]{2,1,0:T(8,128)(2,1)S(1)} %collective-permute-done.8.rest_6_.rest_8_), channel_id=1, source_target_pairs={{0,8},{8,12},{12,4},{4,0},{1,9},{9,13},{13,5},{5,1},{2,10},{10,14}... | collective-permute-start | bytes 786440 | tf_op jit(solution)/shard_map/ppermute | solution.py:359
  48.4 3.6 %copy-start.17 = (bf16[4,64,512]{2,1,0:T(8,128)(2,1)}, bf16[4,64,512]{2,1,0:T(8,128)(2,1)S(1)}, u32[]{:S(2)}) copy-start(bf16[4,64,512]{2,1,0:T(8,128)(2,1)S(1)} %collective-permute-done.4.rest_2_.rest_3_) | copy-start | bytes 786436
  48.4 3.6 %copy-start.15 = (bf16[4,64,512]{2,1,0:T(8,128)(2,1)}, bf16[4,64,512]{2,1,0:T(8,128)(2,1)S(1)}, u32[]{:S(2)}) copy-start(bf16[4,64,512]{2,1,0:T(8,128)(2,1)S(1)} %collective-permute-done.6.rest_4_.rest_5_) | copy-start | bytes 786436
  52.0 0.7 copy-start.19
  52.0 1.0 copy-start.37
  52.0 1.0 copy-start.21
  62.3 35.8 %copy-start.4 = (bf16[4,64,512]{2,1,0:T(8,128)(2,1)S(1)}, bf16[4,64,512]{2,1,0:T(8,128)(2,1)}, u32[]{:S(2)}) copy-start(bf16[4,64,512]{2,1,0:T(8,128)(2,1)} %shard_map.160.rest_0_) | copy-start | bytes 786436
  62.3 35.8 %copy-start.6 = (bf16[4,64,512]{2,1,0:T(8,128)(2,1)S(1)}, bf16[4,64,512]{2,1,0:T(8,128)(2,1)}, u32[]{:S(2)}) copy-start(bf16[4,64,512]{2,1,0:T(8,128)(2,1)} %copy-done.5) | copy-start | bytes 786436
  62.3 35.8 %copy-start.8 = (bf16[128,1024]{1,0:T(8,128)(2,1)S(1)}, bf16[128,1024]{1,0:T(8,128)(2,1)}, u32[]{:S(2)}) copy-start(bf16[128,1024]{1,0:T(8,128)(2,1)} %copy-done.7) | copy-start | bytes 786436
  62.3 35.8 %copy-start.10 = (bf16[4,64,512]{2,1,0:T(8,128)(2,1)S(1)}, bf16[4,64,512]{2,1,0:T(8,128)(2,1)}, u32[]{:S(2)}) copy-start(bf16[4,64,512]{2,1,0:T(8,128)(2,1)} %copy-done.9) | copy-start | bytes 786436
  62.3 35.8 %copy-start.12 = (bf16[4,64,512]{2,1,0:T(8,128)(2,1)S(1)}, bf16[4,64,512]{2,1,0:T(8,128)(2,1)}, u32[]{:S(2)}) copy-start(bf16[4,64,512]{2,1,0:T(8,128)(2,1)} %copy-done.11) | copy-start | bytes 786436
  62.3 35.8 %copy-start.14 = (bf16[4,64,512]{2,1,0:T(8,128)(2,1)S(1)}, bf16[4,64,512]{2,1,0:T(8,128)(2,1)}, u32[]{:S(2)}) copy-start(bf16[4,64,512]{2,1,0:T(8,128)(2,1)} %copy-done.13) | copy-start | bytes 786436
  62.3 35.8 %copy-start.16 = (bf16[4,64,512]{2,1,0:T(8,128)(2,1)S(1)}, bf16[4,64,512]{2,1,0:T(8,128)(2,1)}, u32[]{:S(2)}) copy-start(bf16[4,64,512]{2,1,0:T(8,128)(2,1)} %copy-done.15) | copy-start | bytes 786436
  62.3 35.8 %copy-start.18 = (bf16[4,64,512]{2,1,0:T(8,128)(2,1)S(1)}, bf16[4,64,512]{2,1,0:T(8,128)(2,1)}, u32[]{:S(2)}) copy-start(bf16[4,64,512]{2,1,0:T(8,128)(2,1)} %copy-done.17) | copy-start | bytes 786436
  62.3 35.8 %copy-start.28 = (f32[1024]{0:T(1024)S(1)}, f32[1024]{0:T(1024)}, u32[]{:S(2)}) copy-start(f32[1024]{0:T(1024)} %param.22) | copy-start | bytes 12292
  62.3 35.8 %copy-start.30 = (s32[4,4]{1,0:T(4,128)S(1)}, s32[4,4]{1,0:T(4,128)}, u32[]{:S(2)}) copy-start(s32[4,4]{1,0:T(4,128)} %constant.2.clone.chips) | copy-start | bytes 196
  62.4 2.4 %collective-permute-start.12 = (bf16[320,1024]{1,0:T(8,128)(2,1)}, bf16[320,1024]{1,0:T(8,128)(2,1)S(1)}, u32[]{:S(2)}, u32[]{:S(2)}) collective-permute-start(bf16[320,1024]{1,0:T(8,128)(2,1)} %get-tuple-element.28), channel_id=1, source_target_pairs={{0,1},{1,0},{2,3},{3,2},{4,5},{5,4},{6,7},{7,6},{8,9},{9,8},{10,11... | collective-permute-start | bytes 1966088 | tf_op jit(solution)/shard_map/ppermute | solution.py:272
  64.7 37.7 %copy-start.35 = (s32[2]{0:T(128)S(1)}, s32[2]{0:T(128)}, u32[]{:S(2)}) copy-start(s32[2]{0:T(128)} %copy-done.34) | copy-start | bytes 28
  67.0 22.3 %all-to-all-start.1 = ((bf16[8,40,1024]{2,1,0:T(8,128)(2,1)}), bf16[8,40,1024]{2,1,0:T(8,128)(2,1)S(1)}, u32[]{:S(2)}, u32[]{:S(2)}) async-start(bf16[8,40,1024]{2,1,0:T(8,128)(2,1)} %bitcast.16), calls=%async_computation.1 | async-start | bytes 1310720 | tf_op jit(solution)/shard_map/all_to_all | solution.py:462
  71.2 9.5 %collective-permute-start.16 = (bf16[4,64,512]{2,1,0:T(8,128)(2,1)}, bf16[4,64,512]{2,1,0:T(8,128)(2,1)}, u32[]{:S(2)}, u32[]{:S(2)}) collective-permute-start(bf16[4,64,512]{2,1,0:T(8,128)(2,1)} %copy-done.13), channel_id=1, source_target_pairs={{0,16},{16,0},{1,17},{17,1},{2,18},{18,2},{3,19},{19,3},{4,20},{20... | collective-permute-start | bytes 786440 | tf_op jit(solution)/shard_map/ppermute | solution.py:342
  72.7 14.9 %collective-permute-start.18 = (bf16[4,64,512]{2,1,0:T(8,128)(2,1)}, bf16[4,64,512]{2,1,0:T(8,128)(2,1)}, u32[]{:S(2)}, u32[]{:S(2)}) collective-permute-start(bf16[4,64,512]{2,1,0:T(8,128)(2,1)} %copy-done.21), channel_id=1, source_target_pairs={{0,2},{2,0},{1,3},{3,1},{4,6},{6,4},{5,7},{7,5},{8,10},{10,8},{9,1... | collective-permute-start | bytes 786440 | tf_op jit(solution)/shard_map/ppermute | solution.py:342
  74.7 17.4 %collective-permute-start.14 = (bf16[4,64,512]{2,1,0:T(8,128)(2,1)}, bf16[4,64,512]{2,1,0:T(8,128)(2,1)}, u32[]{:S(2)}, u32[]{:S(2)}) collective-permute-start(bf16[4,64,512]{2,1,0:T(8,128)(2,1)} %copy-done.15), channel_id=1, source_target_pairs={{0,16},{16,0},{1,17},{17,1},{2,18},{18,2},{3,19},{19,3},{4,20},{20... | collective-permute-start | bytes 786440 | tf_op jit(solution)/shard_map/ppermute | solution.py:342
  75.2 17.9 %collective-permute-start.15 = (bf16[4,64,512]{2,1,0:T(8,128)(2,1)}, bf16[4,64,512]{2,1,0:T(8,128)(2,1)}, u32[]{:S(2)}, u32[]{:S(2)}) collective-permute-start(bf16[4,64,512]{2,1,0:T(8,128)(2,1)} %copy-done.13), channel_id=1, source_target_pairs={{0,2},{2,0},{1,3},{3,1},{4,6},{6,4},{5,7},{7,5},{8,10},{10,8},{9,1... | collective-permute-start | bytes 786440 | tf_op jit(solution)/shard_map/ppermute | solution.py:342
  75.2 22.8 %collective-permute-start.19 = (bf16[4,64,512]{2,1,0:T(8,128)(2,1)}, bf16[4,64,512]{2,1,0:T(8,128)(2,1)}, u32[]{:S(2)}, u32[]{:S(2)}) collective-permute-start(bf16[4,64,512]{2,1,0:T(8,128)(2,1)} %copy-done.21), channel_id=1, source_target_pairs={{0,16},{16,0},{1,17},{17,1},{2,18},{18,2},{3,19},{19,3},{4,20},{20... | collective-permute-start | bytes 786440 | tf_op jit(solution)/shard_map/ppermute | solution.py:342
  80.7 17.4 %collective-permute-start.17 = (bf16[4,64,512]{2,1,0:T(8,128)(2,1)}, bf16[4,64,512]{2,1,0:T(8,128)(2,1)}, u32[]{:S(2)}, u32[]{:S(2)}) collective-permute-start(bf16[4,64,512]{2,1,0:T(8,128)(2,1)} %collective-permute-done.16.rest_10_), channel_id=1, source_target_pairs={{0,2},{2,0},{1,3},{3,1},{4,6},{6,4},{5,7},{7,5},{8,10},{10,8},{9,1... | collective-permute-start | bytes 786440 | tf_op jit(solution)/shard_map/ppermute | solution.py:342
  87.5 10.5 %collective-permute-start.20 = (bf16[4,64,512]{2,1,0:T(8,128)(2,1)}, bf16[4,64,512]{2,1,0:T(8,128)(2,1)}, u32[]{:S(2)}, u32[]{:S(2)}) collective-permute-start(bf16[4,64,512]{2,1,0:T(8,128)(2,1)} %collective-permute-done.18.rest_13_), channel_id=1, source_target_pairs={{0,16},{16,0},{1,17},{17,1},{2,18},{18,2},{3,19},{19,3},{4,20},{20... | collective-permute-start | bytes 786440 | tf_op jit(solution)/shard_map/ppermute | solution.py:342
  89.2 0.9 copy-start.25
  90.1 0.9 copy-start.27
  92.2 10.2 %collective-permute-start.13 = (bf16[128,1024]{1,0:T(8,128)(2,1)}, bf16[128,1024]{1,0:T(8,128)(2,1)S(1)}, u32[]{:S(2)}, u32[]{:S(2)}) collective-permute-start(bf16[128,1024]{1,0:T(8,128)(2,1)} %get-tuple-element.20), channel_id=1, source_target_pairs={{0,1},{1,0},{2,3},{3,2},{4,5},{5,4},{6,7},{7,6},{8,9},{9,8},{10,11... | collective-permute-start | bytes 786440 | tf_op jit(solution)/shard_map/ppermute | solution.py:272
  98.1 1.0 copy-start.20
  99.1 0.9 copy-start.22
  100.0 6.9 %copy-start.33 = (s32[2]{0:T(128)S(1)}, s32[2]{0:T(128)}, u32[]{:S(2)}) copy-start(s32[2]{0:T(128)} %tgt_lengths.1) | copy-start | bytes 28
  105.3 1.6 %collective-permute-start.21 = (bf16[128,1024]{1,0:T(8,128)(2,1)S(1)}, bf16[128,1024]{1,0:T(8,128)(2,1)S(1)}, u32[]{:S(2)}, u32[]{:S(2)}) collective-permute-start(bf16[128,1024]{1,0:T(8,128)(2,1)S(1)} %get-tuple-element.41), channel_id=1, source_target_pairs={{0,1},{1,0},{2,3},{3,2},{4,5},{5,4},{6,7},{7,6},{8,9},{9,8},{10,11... | collective-permute-start | bytes 786440 | tf_op jit(solution)/shard_map/ppermute | solution.py:272
